TPU v7x, 512 devices: a whole 4x8x8 slice. The times are simulated.
512 devices in a mesh: kpt: 8 (over x, core), orb: 64 (over y, z).
Axes of the slice: x: 4, y: 8, z: 8, core: 2. Of those that a mesh axis runs over, the one named last changes fastest.
Arguments:
- wavefunctions: float32 [8, 64, 102400], P('kpt', 'orb'), may hold values from -8 to 8
- kpoint_vector: float32 [8, 3], P('kpt'), may hold values from -1 to 1
- kpoint_weight: float32 [8], P('kpt'), may hold values from 0.05 to 0.3
- occupation: float32 [48], replicated, may hold values from 0.25 to 2
- orbital_slot: int32 [48], replicated, may hold values from 0 to 63, as said below
- piece_rows: int32 [64], replicated, may hold values from 1 to 20, 640 in all
- external_potential: float32 [8, 6400], P(None, 'orb'), may hold values from -6 to 6
- core_density: float32 [8, 6400], P(None, 'orb'), may hold values from 0.1 to 4
Outputs:
- density: float32 [8, 6400], P(None, 'orb')
- new_orbitals: float32 [8, 48, 204800], P('kpt', None, 'orb')
Inputs may be any that keep to these rules, and one draw needn't show every extreme that they name: `orbital_slot`: distinct slot numbers; 0 and 63 are always among them. `piece_rows`: the entries sum to 640.
All inputs are finite; a program needn't handle non-finite values.
Results may differ from a plain program's by a relative error of at most 0.00013.
Values sent between devices are 32-bit elements; how exact they have to be, the bound alone decides.
No kernel may reach another device: no remote copies, remote signals or barrier semaphores. Data moves between devices by JAX's collectives and lax.ppermute only.
A program may use at most 64 MiB of HBM per device.

v0:
```python
import math

import jax
import jax.numpy as jnp
import numpy as np
from jax import lax
from jax.sharding import PartitionSpec as P

NX = 80
NY = 80
NZ = 8


magic_taps = (
    8.433424733352934e-07,
    -1.290557201342061e-05,
    8.76298447621056e-05,
    -0.00030158038132690465,
    0.001747237136729939,
    -0.009420470302010804,
    0.023738214637249424,
    0.0612625895831208,
    0.9940415697834004,
    -0.06048952891969835,
    -0.021030251609303816,
    0.013372634148547948,
    -0.0034412814449349387,
    0.0004944322768868992,
    -5.185986881173433e-05,
    2.7273449291197967e-06,
)
grid_step = 0.9
half_order = 14
spectrum_center = 13.0
spectrum_half = 17.0
exchange_coef = (3.0 / math.pi) ** (1.0 / 3.0)
exact_mode = lax.Precision.HIGHEST


def stencil_taps():
    factorial = math.factorial
    second_taps = {}
    first_taps = {}
    running = 0.0
    for offset in range(1, half_order + 1):
        weight_j = factorial(half_order) ** 2 / (
            factorial(half_order - offset) * factorial(half_order + offset)
        )
        tap_sign = (-1.0) ** (offset + 1)
        second_taps[offset] = 2.0 * tap_sign * weight_j / offset**2
        second_taps[-offset] = second_taps[offset]
        first_taps[offset] = tap_sign * weight_j / offset
        first_taps[-offset] = -first_taps[offset]
        running = running + 2.0 * second_taps[offset]
    second_taps[0] = -running
    return (second_taps, first_taps)


def band_matrix(length, taps):
    matrix = np.zeros((length, length))
    for offset, tap_value in taps.items():
        matrix = matrix + tap_value * np.eye(length, k=offset)
    return matrix


def axis_tables(length):
    second_taps, first_taps = stencil_taps()
    magic_band = band_matrix(
        length, {tap_index - 8: magic_taps[tap_index] for tap_index in range(16)}
    )
    return (
        band_matrix(length, second_taps) * (-0.5 / grid_step**2),
        band_matrix(length, first_taps) / grid_step,
        magic_band,
    )


def apply_last(grid_field, matrix):
    return jnp.einsum("azyc,dc->azyd", grid_field, matrix, precision=exact_mode)


def apply_rows(grid_field, matrix):
    return jnp.einsum("wy,azyc->azwc", matrix, grid_field, precision=exact_mode)


def apply_planes(grid_field, matrix):
    return jnp.einsum("vz,azyc->avyc", matrix, grid_field, precision=exact_mode)


def swap_halves(values):
    half_width = values.shape[-1] // 2
    return jnp.concatenate([values[..., half_width:], -values[..., :half_width]], axis=-1)


def magic_tables(grid_field):
    half_width = grid_field.shape[3] // 2
    magic_x = jnp.asarray(np.kron(np.eye(2), axis_tables(half_width)[2]), jnp.float32)
    magic_y = jnp.asarray(axis_tables(grid_field.shape[2])[2], jnp.float32)
    magic_z = jnp.asarray(axis_tables(grid_field.shape[1])[2], jnp.float32)
    return (magic_x, magic_y, magic_z)


def magic_forward(grid_field):
    magic_x, magic_y, magic_z = magic_tables(grid_field)
    smooth = apply_last(grid_field, magic_x)
    smooth = apply_rows(smooth, magic_y)
    return apply_planes(smooth, magic_z)


def magic_backward(grid_field):
    magic_x, magic_y, magic_z = magic_tables(grid_field)
    coarse = apply_planes(grid_field, magic_z.T)
    coarse = apply_rows(coarse, magic_y.T)
    return apply_last(coarse, magic_x.T)


def kinetic(grid_field, wave_vector):
    half_width = grid_field.shape[3] // 2
    tables_x = axis_tables(half_width)
    tables_y = axis_tables(grid_field.shape[2])
    tables_z = axis_tables(grid_field.shape[1])
    twist_table = np.array([[0.0, 1.0], [-1.0, 0.0]])
    along_x = jnp.asarray(np.kron(np.eye(2), tables_x[0]), jnp.float32)
    along_x = along_x + wave_vector[0] * jnp.asarray(np.kron(twist_table, tables_x[1]), jnp.float32)
    along_x = along_x + 0.5 * jnp.sum(wave_vector * wave_vector) * jnp.eye(
        2 * half_width, dtype=jnp.float32
    )
    stack_y = jnp.stack(
        [
            jnp.asarray(tables_y[0], jnp.float32),
            wave_vector[1] * jnp.asarray(tables_y[1], jnp.float32),
        ]
    )
    stack_z = jnp.stack(
        [
            jnp.asarray(tables_z[0], jnp.float32),
            wave_vector[2] * jnp.asarray(tables_z[1], jnp.float32),
        ]
    )
    parts_y = jnp.einsum("swy,azyc->sazwc", stack_y, grid_field, precision=exact_mode)
    parts_z = jnp.einsum("svz,azyc->savyc", stack_z, grid_field, precision=exact_mode)
    return (
        apply_last(grid_field, along_x)
        + parts_y[0]
        + parts_z[0]
        + swap_halves(parts_y[1] + parts_z[1])
    )


def potential_pair(potential, planes, rows_y):
    shaped = potential.reshape(planes, rows_y, -1)
    return jnp.concatenate([shaped, shaped], axis=-1)


def chebyshev_image(grid_field, smooth, pair_field, wave_vector):
    applied = kinetic(grid_field, wave_vector) + magic_backward(pair_field[None] * smooth)
    first_term = (applied - spectrum_center * grid_field) / spectrum_half
    applied_again = kinetic(first_term, wave_vector) + magic_backward(
        pair_field[None] * magic_forward(first_term)
    )
    return applied_again - spectrum_center * first_term


def split_stack(pieces):
    orbital_count, row_count, double_width = pieces.shape
    half_width = double_width // 2
    return (
        pieces.reshape(orbital_count, row_count, 2, half_width)
        .transpose(2, 0, 1, 3)
        .reshape(2 * orbital_count, row_count * half_width)
    )


def gram_of(stacked):
    return jnp.dot(stacked, stacked.T, precision=exact_mode, preferred_element_type=jnp.float32)


def rotate_with(gram_matrix, stacked, components, half_width):
    orbital_count = gram_matrix.shape[0] // 2
    gram_aa = gram_matrix[:orbital_count, :orbital_count]
    gram_ab = gram_matrix[:orbital_count, orbital_count:]
    gram_ba = gram_matrix[orbital_count:, :orbital_count]
    gram_bb = gram_matrix[orbital_count:, orbital_count:]
    over_real = gram_aa + gram_bb
    over_imag = gram_ab - gram_ba
    mean_square = jnp.trace(over_real) / (orbital_count * components) + 1e-06
    shrink_factor = 0.5 / (components * mean_square)
    rot_real = 1.5 * jnp.eye(orbital_count, dtype=jnp.float32) - shrink_factor * over_real
    rot_imag = -shrink_factor * over_imag
    rotation = jnp.concatenate(
        [jnp.concatenate([rot_real, rot_imag], 1), jnp.concatenate([-rot_imag, rot_real], 1)], 0
    )
    new_stack = jnp.dot(
        rotation.T, stacked, precision=exact_mode, preferred_element_type=jnp.float32
    ) / jnp.sqrt(mean_square)
    row_count = stacked.shape[1] // half_width
    return (
        new_stack.reshape(2, orbital_count, row_count, half_width)
        .transpose(1, 2, 0, 3)
        .reshape(orbital_count, row_count, 2 * half_width)
    )


def on_device(
    wavefunctions,
    kpoint_vector,
    kpoint_weight,
    occupation,
    orbital_slot,
    piece_rows,
    external_potential,
    core_density,
):
    slot_count = wavefunctions.shape[1]
    rank_count = lax.axis_size("orb")
    own_index = lax.axis_index("orb")
    capacity = 2 * NZ * NY // rank_count
    flat_width = rank_count * capacity * 2 * NX
    grid_field = wavefunctions[0].reshape(slot_count, NZ, NY, 2 * NX)
    wave_vector = kpoint_vector[0]
    offsets = jnp.cumsum(piece_rows) - piece_rows
    positions = jnp.minimum(
        offsets[:, None] + jnp.arange(capacity, dtype=jnp.int32)[None, :], NZ * NY - 1
    ).reshape(-1)
    slot_ids = own_index * slot_count + jnp.arange(slot_count, dtype=jnp.int32)
    matches = (orbital_slot[:, None] == slot_ids[None, :]).astype(jnp.float32)
    slot_occupation = jnp.sum(matches * occupation[:, None], axis=0)
    smooth = magic_forward(grid_field)
    squares = smooth[..., :NX] ** 2 + smooth[..., NX:] ** 2
    partial_density = (
        kpoint_weight[0] * jnp.sum(slot_occupation[:, None, None, None] * squares, axis=0)
    ).reshape(NZ, NY * NX)
    box_total = lax.psum(partial_density, "kpt")
    slab_density = lax.psum_scatter(box_total, "orb", scatter_dimension=1, tiled=True)
    slab_potential = external_potential - exchange_coef * jnp.power(
        slab_density + core_density, 1.0 / 3.0
    )
    potential = lax.all_gather(slab_potential, "orb", axis=1, tiled=True)
    pair_field = potential_pair(potential, NZ, NY)
    image_field = chebyshev_image(grid_field, smooth, pair_field, wave_vector)
    filtered_rows = (2.0 * image_field / spectrum_half - grid_field).reshape(
        slot_count, NZ * NY, 2 * NX
    )
    filtered_flat = jnp.take(filtered_rows, positions, axis=1).reshape(slot_count, flat_width)
    received = lax.all_to_all(filtered_flat, "orb", split_axis=1, concat_axis=1, tiled=True)
    grouped = received.reshape(slot_count, rank_count, capacity, 2 * NX)
    pieces = grouped[orbital_slot % slot_count, orbital_slot // slot_count]
    live_rows = jnp.arange(capacity, dtype=jnp.int32) < piece_rows[own_index]
    pieces = jnp.where(live_rows[None, :, None], pieces, 0.0)
    stacked = split_stack(pieces)
    gram_matrix = lax.psum(gram_of(stacked), "orb")
    new_rows = rotate_with(gram_matrix, stacked, NZ * NY * 2 * NX, NX)
    return (slab_density, new_rows.reshape(new_rows.shape[0], capacity * 2 * NX)[None])


def solution(mesh):
    in_specs = (
        P("kpt", "orb", None),
        P("kpt", None),
        P("kpt"),
        P(),
        P(),
        P(),
        P(None, "orb"),
        P(None, "orb"),
    )
    out_specs = (P(None, "orb"), P("kpt", None, "orb"))
    return jax.shard_map(
        on_device, mesh=mesh, in_specs=in_specs, out_specs=out_specs, check_vma=False
    )
```

profile of v0, /device:TPU:32, one launch (start us, length us, event | category | flops | bytes accessed | tf_op | source)
XLA Modules:
  0.0 594.0 jit_solution(3185467553066338049)
XLA Ops:
  7.7 2.6 reduce.12
  10.7 1.0 convolution_bitcast_fusion.11
  14.8 0.8 fusion.31
  15.8 0.8 mul.116
  17.2 0.7 multiply_reduce_fusion
  19.2 1.4 fusion.19
  21.0 1.3 reshape.330
  22.3 1.4 multiply_bitcast_fusion.1
  23.7 2.0 convolution_bitcast_fusion.1
  25.8 1.2 slice_bitcast_fusion.5
  27.3 1.6 broadcast_in_dim.42
  29.6 1.3 dynamic-slice
  31.5 2.7 fusion.2
  34.3 136.5 %all-reduce.4.cloned.1.call-done = f32[8,6400]{1,0:T(8,128)} async-done(((f32[8,6400]{1,0:T(8,128)}), f32[8,6400]{1,0:T(8,128)}) %all-reduce.4.cloned.1.call-update) | async-done | bytes 204816
  170.8 0.8 constant_dynamic-slice_fusion
  171.6 12.4 %psum.16 = f32[8,100]{1,0:T(8,128)S(1)} all-reduce(f32[8,100]{1,0:T(8,128)S(1)} %constant_dynamic-slice_fusion), channel_id=1, replica_groups=mesh['kpt'=8,'orb'=64] {'kpt'}, use_global_device_ids=true, to_apply=%region_1.2 | all-reduce | flops 800 | bytes 6400 | tf_op jit(solution)/shard_map/psum | solution.py:233
  184.0 0.7 subtract_bitcast_fusion
  184.7 48.2 %all-gather = f32[64,100,8]{1,2,0:T(8,128)S(1)} all-gather(f32[1,100,8]{1,2,0:T(8,128)S(1)} %subtract_bitcast_fusion), channel_id=1, replica_groups=mesh['kpt'=8,'orb'=64] {'orb'}, dimensions={0}, use_global_device_ids=true | all-gather | bytes 208000 | tf_op jit(solution)/shard_map/all_gather | solution.py:238
  233.6 0.9 convolution_bitcast_fusion.7
  234.4 1.5 convolution_bitcast_fusion.6
  236.0 1.6 fusion.3
  237.6 0.7 copy-done.9
  238.3 1.2 convolution_bitcast_fusion
  239.5 1.1 fusion.24
  240.6 1.5 fusion.17
  242.0 0.8 copy.145
  242.9 0.8 slice_bitcast_fusion.4
  243.7 1.5 convolution_bitcast_fusion.5
  245.3 2.3 copy.106
  247.6 1.8 fusion.10
  249.4 0.7 convolution_bitcast_fusion.3
  250.2 12.6 %convolution_bitcast_fusion.2 = f32[8,80,160]{1,2,0:T(8,128)S(1)} fusion(f32[80,80,1]{1,0,2:T(8,128)S(1)} %copy-done.8, f32[8,80,160]{2,0,1:T(8,128)S(1)} %convolution_bitcast_fusion.3), kind=kOutput, calls=%fused_computation.10 | convolution fusion | flops 98304000 | bytes 844800 | tf_op jit(solution)/shard_map/wy,azyc->azwc/dot_general | solution.py:83
  262.8 1.3 fusion.5
  264.1 1.6 fusion.8
  265.6 3.2 gather_fusion
  268.8 0.8 gather.12
  269.8 1.7 copy.110
  271.6 11.4 %all-to-all-start = ((f32[1,64,3200]{2,0,1:T(1,128)}), f32[1,64,3200]{2,0,1:T(1,128)S(1)}, u32[]{:S(2)}, u32[]{:S(2)}) async-start(f32[1,64,3200]{2,0,1:T(1,128)} %copy.110), calls=%async_computation | async-start | bytes 1638400 | tf_op jit(solution)/shard_map/all_to_all | solution.py:245
  284.2 14.1 %all-to-all-done = f32[1,64,3200]{2,0,1:T(1,128)S(1)} async-done(((f32[1,64,3200]{2,0,1:T(1,128)}), f32[1,64,3200]{2,0,1:T(1,128)S(1)}, u32[]{:S(2)}, u32[]{:S(2)}) %all-to-all-start) | async-done | bytes 819232 | tf_op jit(solution)/shard_map/all_to_all | solution.py:245
  298.3 1.9 reduce.7
  300.2 0.8 reshape.296
  301.0 0.7 gather_fusion.1
  303.9 0.7 fusion.71
  304.6 276.7 %psum.15 = f32[96,96]{1,0:T(8,128)S(1)} all-reduce(f32[96,96]{1,0:T(8,128)S(1)} %fusion.71), channel_id=1, replica_groups=mesh['kpt'=8,'orb'=64] {'orb'}, use_global_device_ids=true, to_apply=%region_5.6 | all-reduce | flops 9216 | bytes 73728 | tf_op jit(solution)/shard_map/psum | solution.py:251
  581.3 0.7 select_reduce_fusion
  582.8 0.8 convolution_divide_fusion
  584.1 0.8 copy.113
  584.9 2.1 broadcast_in_dim_reshape_reshape.3
  (81 shorter events, 10.9 us)
Async XLA Ops:
  7.2 3.5 copy-start.3
  7.2 163.6 %all-reduce.4.cloned.1.call-start = ((), (), s32[]{:S(2)}) async-start(), calls=%async_computation.1 | async-start | bytes 409600
  10.4 1.4 copy-start.8
  11.7 1.8 copy-start.10
  12.4 1.8 copy-start.18
  12.4 1.8 copy-start.19
  14.2 2.4 copy-start.13
  14.2 3.7 copy-start.16
  14.8 3.7 copy-start.14
  14.8 4.3 copy-start.11
  25.7 1.3 copy-start.2
  31.5 152.5 %copy-start.15 = (f32[8,100]{1,0:T(8,128)S(1)}, f32[8,100]{1,0:T(8,128)}, u32[]{:S(2)}) copy-start(f32[8,100]{1,0:T(8,128)} %param.38) | copy-start | bytes 9604
  184.0 50.5 %copy-start.12 = (f32[8,100]{1,0:T(8,128)}, f32[8,100]{1,0:T(8,128)S(1)}, u32[]{:S(2)}) copy-start(f32[8,100]{1,0:T(8,128)S(1)} %psum.16) | copy-start | bytes 9604
  237.5 0.8 copy-start.9
  239.5 3.3 copy-start
  249.4 13.4 %copy-start.1 = (f32[2,1,8,80,160]{4,3,2,1,0:T(8,128)S(1)}, f32[2,1,8,80,160]{4,3,2,1,0:T(8,128)}, u32[]{:S(2)}) copy-start(f32[2,1,8,80,160]{4,3,2,1,0:T(8,128)} %copy-done) | copy-start | bytes 2457604
  249.4 13.4 %copy-start.4 = (f32[8,80,80]{2,1,0:T(8,128)S(1)}, f32[8,80,80]{2,1,0:T(8,128)}, u32[]{:S(2)}) copy-start(f32[8,80,80]{2,1,0:T(8,128)} %get-tuple-element.5) | copy-start | bytes 614404
  249.4 13.4 %copy-start.6 = (f32[160,160]{1,0:T(8,128)S(1)}, f32[160,160]{1,0:T(8,128)}, u32[]{:S(2)}) copy-start(f32[160,160]{1,0:T(8,128)} %constant.109.clone) | copy-start | bytes 307204
  249.4 13.4 %copy-start.7 = (f32[160,160]{1,0:T(8,128)S(1)}, f32[160,160]{1,0:T(8,128)}, u32[]{:S(2)}) copy-start(f32[160,160]{1,0:T(8,128)} %constant.110.clone) | copy-start | bytes 307204
  268.8 0.9 copy-start.5
  269.8 13.1 %copy-start.17 = (s32[64]{0:T(128)S(1)}, s32[64]{0:T(128)}, u32[]{:S(2)}) copy-start(s32[64]{0:T(128)} %param.37) | copy-start | bytes 772
  269.8 14.4 %copy-start.20 = (s32[48]{0:T(128)S(1)}, s32[48]{0:T(128)}, u32[]{:S(2)}) copy-start(s32[48]{0:T(128)} %param.36) | copy-start | bytes 580
  271.6 26.7 %all-to-all-start = ((f32[1,64,3200]{2,0,1:T(1,128)}), f32[1,64,3200]{2,0,1:T(1,128)S(1)}, u32[]{:S(2)}, u32[]{:S(2)}) async-start(f32[1,64,3200]{2,0,1:T(1,128)} %copy.110), calls=%async_computation | async-start | bytes 1638400 | tf_op jit(solution)/shard_map/all_to_all | solution.py:245
Sparse Core Ops, SparseCore 0:
  16.7 154.0 all-reduce.3
where the time goes:
time: 597 us; the launch traced here: 594 us
  blocking collectives  337 us (56%)
  waiting for transfers between devices  151 us (25%)
  matrix products  37.1 us (6%)
  local copies, waits for them, and re-layouts  25.9 us (4%)
  between operations  17.6 us (3%)
  other arithmetic  14.1 us (2%)
  starting transfers between devices  11.4 us (2%)
    psum x1, blocking collectives, on_device(): gram_matrix = lax.psum(gram_of(stacked), 'orb')  277 us
    unnamed x2, waiting for transfers between devices  137 us
    all_gather x1, blocking collectives, on_device(): potential = lax.all_gather(slab_potential, 'orb', axis=1, tiled=True)  48.2 us
    dot_general x4, matrix products, apply_rows(): return jnp.einsum('wy,azyc->azwc', matrix, grid_field, precision=exact_mode)  16.3 us
    all_to_all x1, waiting for transfers between devices, on_device(): lax.all_to_all(filtered_flat, 'orb', split_axis=1, concat_axis=1, tiled=T...  14.1 us
    psum x1, blocking collectives, on_device(): box_total = lax.psum(partial_density, 'kpt')  12.4 us
  transfers between devices with their start and end apart: 2, of which 2 were waited for; matrix products, arithmetic and copies ran while one was open for 3% of the time, Pallas kernels for 0%

commit v1 on v0

--- a/solution.py
+++ b/solution.py
@@ -4,12 +4,12 @@
 import jax.numpy as jnp
 import numpy as np
 from jax import lax
+from jax.sharding import Mesh
 from jax.sharding import PartitionSpec as P
 
 NX = 80
 NY = 80
 NZ = 8
-
 
 magic_taps = (
     8.433424733352934e-07,
@@ -171,34 +171,12 @@
     )
 
 
-def gram_of(stacked):
-    return jnp.dot(stacked, stacked.T, precision=exact_mode, preferred_element_type=jnp.float32)
-
-
-def rotate_with(gram_matrix, stacked, components, half_width):
-    orbital_count = gram_matrix.shape[0] // 2
-    gram_aa = gram_matrix[:orbital_count, :orbital_count]
-    gram_ab = gram_matrix[:orbital_count, orbital_count:]
-    gram_ba = gram_matrix[orbital_count:, :orbital_count]
-    gram_bb = gram_matrix[orbital_count:, orbital_count:]
-    over_real = gram_aa + gram_bb
-    over_imag = gram_ab - gram_ba
-    mean_square = jnp.trace(over_real) / (orbital_count * components) + 1e-06
-    shrink_factor = 0.5 / (components * mean_square)
-    rot_real = 1.5 * jnp.eye(orbital_count, dtype=jnp.float32) - shrink_factor * over_real
-    rot_imag = -shrink_factor * over_imag
-    rotation = jnp.concatenate(
-        [jnp.concatenate([rot_real, rot_imag], 1), jnp.concatenate([-rot_imag, rot_real], 1)], 0
-    )
-    new_stack = jnp.dot(
-        rotation.T, stacked, precision=exact_mode, preferred_element_type=jnp.float32
-    ) / jnp.sqrt(mean_square)
-    row_count = stacked.shape[1] // half_width
-    return (
-        new_stack.reshape(2, orbital_count, row_count, half_width)
-        .transpose(1, 2, 0, 3)
-        .reshape(orbital_count, row_count, 2 * half_width)
-    )
+def exchange(values, axes):
+    return lax.all_to_all(values, axes, split_axis=0, concat_axis=0, tiled=True)
+
+
+def share(values, count, axes):
+    return exchange(jnp.broadcast_to(values[None], (count,) + values.shape), axes)
 
 
 def on_device(
@@ -211,60 +189,88 @@
     external_potential,
     core_density,
 ):
-    slot_count = wavefunctions.shape[1]
-    rank_count = lax.axis_size("orb")
-    own_index = lax.axis_index("orb")
+    kpt, orb = ("kpt",), ("orb_y", "orb_z")
+    kpt_count = lax.axis_size(kpt)
+    rank_count = lax.axis_size(orb)
+    own_index = lax.axis_index(orb)
+    orbital_count = orbital_slot.shape[0]
     capacity = 2 * NZ * NY // rank_count
-    flat_width = rank_count * capacity * 2 * NX
-    grid_field = wavefunctions[0].reshape(slot_count, NZ, NY, 2 * NX)
+    slab = NY * NX // rank_count
+    grid_field = wavefunctions[0].reshape(1, NZ, NY, 2 * NX)
     wave_vector = kpoint_vector[0]
-    offsets = jnp.cumsum(piece_rows) - piece_rows
+    ranks = jnp.arange(rank_count, dtype=jnp.int32)
+    offsets = jnp.sum(
+        jnp.where(ranks[None, :] < ranks[:, None], piece_rows[None, :], 0), axis=1
+    )
     positions = jnp.minimum(
         offsets[:, None] + jnp.arange(capacity, dtype=jnp.int32)[None, :], NZ * NY - 1
     ).reshape(-1)
-    slot_ids = own_index * slot_count + jnp.arange(slot_count, dtype=jnp.int32)
-    matches = (orbital_slot[:, None] == slot_ids[None, :]).astype(jnp.float32)
-    slot_occupation = jnp.sum(matches * occupation[:, None], axis=0)
+    own_occupation = jnp.sum(jnp.where(orbital_slot == own_index, occupation, 0.0))
     smooth = magic_forward(grid_field)
-    squares = smooth[..., :NX] ** 2 + smooth[..., NX:] ** 2
-    partial_density = (
-        kpoint_weight[0] * jnp.sum(slot_occupation[:, None, None, None] * squares, axis=0)
-    ).reshape(NZ, NY * NX)
-    box_total = lax.psum(partial_density, "kpt")
-    slab_density = lax.psum_scatter(box_total, "orb", scatter_dimension=1, tiled=True)
+    squares = smooth[0, ..., :NX] ** 2 + smooth[0, ..., NX:] ** 2
+    partial_density = (kpoint_weight[0] * own_occupation * squares).reshape(NZ, rank_count, slab)
+    by_owner = partial_density.transpose(1, 0, 2).reshape(rank_count, NZ * slab)
+    own_density = jnp.sum(exchange(by_owner, orb), axis=0)
+    own_density = jnp.sum(share(own_density, kpt_count, kpt), axis=0)
+    slab_density = own_density.reshape(NZ, slab)
     slab_potential = external_potential - exchange_coef * jnp.power(
         slab_density + core_density, 1.0 / 3.0
     )
-    potential = lax.all_gather(slab_potential, "orb", axis=1, tiled=True)
+    potential = share(slab_potential.reshape(NZ * slab), rank_count, orb)
+    potential = potential.reshape(rank_count, NZ, slab).transpose(1, 0, 2).reshape(NZ, NY * NX)
     pair_field = potential_pair(potential, NZ, NY)
     image_field = chebyshev_image(grid_field, smooth, pair_field, wave_vector)
-    filtered_rows = (2.0 * image_field / spectrum_half - grid_field).reshape(
-        slot_count, NZ * NY, 2 * NX
-    )
-    filtered_flat = jnp.take(filtered_rows, positions, axis=1).reshape(slot_count, flat_width)
-    received = lax.all_to_all(filtered_flat, "orb", split_axis=1, concat_axis=1, tiled=True)
-    grouped = received.reshape(slot_count, rank_count, capacity, 2 * NX)
-    pieces = grouped[orbital_slot % slot_count, orbital_slot // slot_count]
-    live_rows = jnp.arange(capacity, dtype=jnp.int32) < piece_rows[own_index]
-    pieces = jnp.where(live_rows[None, :, None], pieces, 0.0)
-    stacked = split_stack(pieces)
-    gram_matrix = lax.psum(gram_of(stacked), "orb")
-    new_rows = rotate_with(gram_matrix, stacked, NZ * NY * 2 * NX, NX)
-    return (slab_density, new_rows.reshape(new_rows.shape[0], capacity * 2 * NX)[None])
+    filtered_rows = (2.0 * image_field / spectrum_half - grid_field).reshape(NZ * NY, 2 * NX)
+    outgoing = jnp.take(filtered_rows, positions, axis=0).reshape(
+        rank_count, capacity * 2 * NX
+    )
+    received = exchange(outgoing, orb)
+    live = (jnp.arange(capacity * 2 * NX, dtype=jnp.int32) // (2 * NX)) < jnp.sum(
+        jnp.where(ranks == own_index, piece_rows, 0)
+    )
+    received = jnp.where(live[None, :], received, 0.0)
+    chosen = (orbital_slot[:, None] == ranks[None, :]).astype(jnp.float32)
+    pieces = jnp.dot(chosen, received, precision=exact_mode)
+    swapped = swap_halves(pieces.reshape(orbital_count, capacity, 2 * NX)).reshape(pieces.shape)
+    stacked = jnp.concatenate([pieces, swapped], axis=0)
+    gram = lax.dot_general(pieces, stacked, (((1,), (1,)), ((), ())), precision=exact_mode)
+    order = jnp.arange(orbital_count)
+    upper = order[:, None] <= order[None, :]
+    packed = jnp.where(upper, gram[:, :orbital_count], gram[:, orbital_count:])
+    packed = packed.reshape(-1)
+    for axis in ("orb_z", "orb_y"):
+        packed = jnp.sum(share(packed, lax.axis_size(axis), (axis,)), axis=0)
+    packed = packed.reshape(orbital_count, orbital_count)
+    over_real = jnp.where(upper, packed, packed.T)
+    over_imag = jnp.where(upper, -packed.T, packed)
+    over_imag = jnp.where(jnp.eye(orbital_count, dtype=bool), 0.0, over_imag)
+    components = NZ * NY * 2 * NX
+    mean_square = jnp.trace(over_real) / (orbital_count * components) + 1e-06
+    shrink_factor = 0.5 / (components * mean_square)
+    rot_real = 1.5 * jnp.eye(orbital_count, dtype=jnp.float32) - shrink_factor * over_real
+    rot_imag = -shrink_factor * over_imag
+    rotation = jnp.concatenate([rot_real.T, -rot_imag.T], axis=1) / jnp.sqrt(mean_square)
+    new_rows = jnp.dot(rotation, stacked, precision=exact_mode)
+    return (slab_density, new_rows[None])
 
 
 def solution(mesh):
+    side = math.isqrt(mesh.shape["orb"])
+    fine = Mesh(
+        mesh.devices.reshape(mesh.shape["kpt"], -1, side), ("kpt", "orb_y", "orb_z")
+    )
+    orb = ("orb_y", "orb_z")
     in_specs = (
-        P("kpt", "orb", None),
+        P("kpt", orb, None),
         P("kpt", None),
         P("kpt"),
         P(),
         P(),
         P(),
-        P(None, "orb"),
-        P(None, "orb"),
-    )
-    out_specs = (P(None, "orb"), P("kpt", None, "orb"))
+        P(None, orb),
+        P(None, orb),
+    )
+    out_specs = (P(None, orb), P("kpt", None, orb))
     return jax.shard_map(
-        on_device, mesh=mesh, in_specs=in_specs, out_specs=out_specs, check_vma=False
-    )
+        on_device, mesh=fine, in_specs=in_specs, out_specs=out_specs, check_vma=False
+    )

time: 597 us -> 169 us (0.28)
  the two profiles are of different devices: /device:TPU:32 before, /device:TPU:2 now
where the time goes in v1:
time: 169 us; the launch traced here: 168 us
  starting transfers between devices  38 us (22%)
  waiting for transfers between devices  35.9 us (21%)
  matrix products  28.4 us (17%)
  blocking collectives  24.1 us (14%)
  local copies, waits for them, and re-layouts  22.1 us (13%)
  other arithmetic  15.1 us (9%)
  between operations  4.05 us (2%)
    all_to_all x4, starting transfers between devices, exchange(): return lax.all_to_all(values, axes, split_axis=0, concat_axis=0, tiled=True)  38 us
    all_to_all x4, waiting for transfers between devices, exchange(): return lax.all_to_all(values, axes, split_axis=0, concat_axis=0, tiled=True)  35.9 us
    all_to_all x2, blocking collectives, exchange(): return lax.all_to_all(values, axes, split_axis=0, concat_axis=0, tiled=True)  24.1 us
    dot_general x6, matrix products, apply_last(): return jnp.einsum('azyc,dc->azyd', grid_field, matrix, precision=exact_mode)  9.32 us
    dot_general x4, matrix products, apply_rows(): return jnp.einsum('wy,azyc->azwc', matrix, grid_field, precision=exact_mode)  5.26 us
    dot_general x4, matrix products, apply_planes(): return jnp.einsum('vz,azyc->avyc', matrix, grid_field, precision=exact_mode)  4.29 us
    gather x2, local copies, waits for them, and re-layouts, on_device(): jnp.take(filtered_rows, positions, axis=0)  3.95 us
  transfers between devices with their start and end apart: 4, of which 4 were waited for; matrix products, arithmetic and copies ran while one was open for 10% of the time, Pallas kernels for 0%

profile of v1, /device:TPU:2, one launch (start us, length us, event | category | flops | bytes accessed | tf_op | source)
XLA Modules:
  0.0 167.6 jit_solution(2710350533751316973)
XLA Ops:
  1.2 2.6 %reduce.13 = f32[102400]{0:T(1024)S(1)} reduce(f32[1,1,102400]{2,1,0:T(1,128)} %param.32, f32[]{:T(128)} %broadcast.153), dimensions={0,1}, to_apply=%param.32.reduce_sub_computation.5 | reduce | bytes 819204 | tf_op args[0]
  4.1 1.0 convolution_bitcast_fusion.12
  9.5 1.1 all_to_all.36
  10.6 16.8 %all-to-all-start = ((f32[64,1,800]{2,1,0:T(1,128)}), f32[64,1,800]{2,1,0:T(1,128)}, u32[]{:S(2)}, u32[]{:S(2)}) async-start(f32[64,1,800]{2,1,0:T(1,128)} %all_to_all.36), calls=%async_computation | async-start | bytes 458752 | tf_op jit(solution)/shard_map/all_to_all | solution.py:175
  29.3 1.4 fusion.21
  31.1 1.3 reshape.314
  32.6 1.4 multiply_bitcast_fusion.1
  34.0 2.0 %convolution_bitcast_fusion.2 = f32[2,1,8,80,160]{4,3,2,1,0:T(8,128)S(1)} fusion(f32[8,80,160,1]{2,1,0,3:T(8,128)S(1)} %reshape.314, f32[1,80,80]{2,1,0:T(8,128)S(1)} %multiply_bitcast_fusion.1, f32[1,80,80]{2,1,0:T(8,128)} %constant.103), kind=kOutput, calls=%fused_computation.3 | convolution fusion | flops 196620800 | bytes 1280000 | tf_op jit(solution)/shard_map/swy,azyc->sazwc/dot_general | solution.py:140
  36.0 1.1 copy-done
  37.1 0.7 compare_and_fusion
  37.8 0.7 min.22
  38.5 0.7 fusion.62
  39.3 0.9 slice_bitcast_fusion.5
  40.2 1.4 all-to-all-done
  41.6 1.1 reduce_sum.87
  43.3 4.8 %all-to-all-start.1 = ((f32[8,1,800]{2,1,0:T(1,128)}), f32[8,1,800]{2,1,0:T(1,128)S(1)}, u32[]{:S(2)}, u32[]{:S(2)}) async-start(f32[8,1,800]{2,1,0:T(1,128)} %broadcast_in_dim.92), calls=%async_computation.1 | async-start | bytes 57344 | tf_op jit(solution)/shard_map/all_to_all | solution.py:175
  49.0 1.4 broadcast_in_dim.98
  51.1 1.0 all-to-all-done.1
  52.4 0.8 broadcast_in_dim.100
  53.2 11.7 %all-to-all-start.2 = ((f32[64,1,800]{2,1,0:T(1,128)}), f32[64,1,800]{2,1,0:T(1,128)}, u32[]{:S(2)}, u32[]{:S(2)}) async-start(f32[64,1,800]{2,1,0:T(1,128)} %broadcast_in_dim.100), calls=%async_computation.2 | async-start | bytes 458752 | tf_op jit(solution)/shard_map/all_to_all | solution.py:175
  64.9 2.8 %fusion.2 = f32[8,80,160]{2,1,0:T(8,128)S(1)} fusion(f32[8,80,160]{2,1,0:T(8,128)S(1)} %reshape.286, f32[2,1,8,80,160]{4,3,2,1,0:T(8,128)S(1)} %bitcast.218, f32[2,1,8,80,160]{4,3,2,1,0:T(8,128)} %copy-done, f32[8,80,80]{2,1,0:T(8,128)} %get-tuple-element.7, f32[8,80,80]{2,1,0:T(8,128)} %get-tuple-element.6, f32[160,160]{1,0:T(8,128)} %constant.92.clone, ...), kind=kOutput, calls=%fused_computation.21 | convolution fusion | flops 197145600 | bytes 2252808 | tf_op jit(solution)/shard_map/azyc,dc->azyd/dot_general | solution.py:79
  67.7 11.1 %all-to-all-done.2 = f32[64,1,800]{2,1,0:T(1,128)} async-done(((f32[64,1,800]{2,1,0:T(1,128)}), f32[64,1,800]{2,1,0:T(1,128)}, u32[]{:S(2)}, u32[]{:S(2)}) %all-to-all-start.2) | async-done | bytes 204832 | tf_op jit(solution)/shard_map/all_to_all | solution.py:175
  78.8 1.5 reduce.7
  80.9 0.9 convolution_bitcast_fusion.8
  81.8 1.5 convolution_bitcast_fusion.7
  83.3 1.6 fusion.3
  84.9 0.7 copy-done.9
  85.6 1.2 convolution_bitcast_fusion.1
  86.8 1.1 fusion.26
  87.9 1.5 fusion.19
  89.4 0.8 copy.189
  90.3 0.8 slice_bitcast_fusion.4
  91.1 1.5 convolution_bitcast_fusion.6
  92.6 2.3 %copy.148 = f32[8,80,160]{2,0,1:T(8,128)} copy(f32[8,80,160]{1,2,0:T(8,128)} %convolution_bitcast_fusion.6) | data formatting | bytes 819200 | tf_op jit(solution)/shard_map/reshape.47
  94.9 1.8 %fusion.10 = f32[8,80,160]{2,0,1:T(8,128)S(1)} fusion(f32[8,80,160]{2,0,1:T(8,128)} %copy.148, f32[8,8,1]{1,0,2:T(8,128)S(1)} %copy-done.11, f32[8,80,80]{2,0,1:T(8,128)S(1)} %copy.139), kind=kOutput, calls=%fused_computation.29 | convolution fusion | flops 10035200 | bytes 1024256 | tf_op jit(solution)/shard_map/vz,azyc->avyc/dot_general | solution.py:87
  96.8 1.0 convolution_bitcast_fusion.4
  97.7 1.5 convolution_bitcast_fusion.3
  99.3 1.3 fusion.5
  100.6 1.6 fusion.8
  102.2 3.2 %gather_fusion = f32[1280,160]{1,0:T(8,128)S(1)} fusion(f32[640,160]{1,0:T(8,128)S(1)} %bitcast.216, s32[2048]{0:T(1024)S(1)} %pad_clamp_fusion), kind=kCustom, calls=%fused_computation | custom fusion | bytes 1643520 | tf_op jit(solution)/shard_map/jit(_take)/gather | solution.py:224
  105.4 0.8 gather.7
  106.4 1.7 %copy.152 = f32[64,1,3200]{2,1,0:T(1,128)} copy(f32[64,1,3200]{2,0,1:T(8,128)S(1)} %broadcast_select_fusion) | data formatting | bytes 1638400 | tf_op jit(solution)/shard_map/jit(_take)/select_n | solution.py:224
  108.1 4.6 %all-to-all-start.3 = ((f32[64,1,3200]{2,1,0:T(1,128)}), f32[64,1,3200]{2,1,0:T(1,128)S(1)}, u32[]{:S(2)}, u32[]{:S(2)}) async-start(f32[64,1,3200]{2,1,0:T(1,128)} %copy.152), calls=%async_computation.3 | async-start | bytes 1638400 | tf_op jit(solution)/shard_map/all_to_all | solution.py:175
  114.1 22.4 %all-to-all-done.3 = f32[64,1,3200]{2,1,0:T(1,128)S(1)} async-done(((f32[64,1,3200]{2,1,0:T(1,128)}), f32[64,1,3200]{2,1,0:T(1,128)S(1)}, u32[]{:S(2)}, u32[]{:S(2)}) %all-to-all-start.3) | async-done | bytes 819232 | tf_op jit(solution)/shard_map/all_to_all | solution.py:175
  138.6 1.4 fusion.11
  140.2 13.3 %all_to_all.43 = f32[8,1,2304]{2,1,0:T(1,128)S(1)} all-to-all(f32[8,1,2304]{2,1,0:T(1,128)S(1)} %broadcast_in_dim.105), channel_id=1, replica_groups=mesh['kpt'=8,'orb_y'=8,'orb_z'=8] {'orb_z'}, dimensions={0} | all-to-all | bytes 147456 | tf_op jit(solution)/shard_map/all_to_all | solution.py:175
  153.6 10.8 %all_to_all.44 = f32[8,1,2304]{2,1,0:T(1,128)S(1)} all-to-all(f32[8,1,2304]{2,1,0:T(1,128)S(1)} %broadcast_in_dim.106), channel_id=1, replica_groups=mesh['kpt'=8,'orb_y'=8,'orb_z'=8] {'orb_y'}, dimensions={0} | all-to-all | bytes 147456 | tf_op jit(solution)/shard_map/all_to_all | solution.py:175
  166.1 1.6 convolution_bitcast_fusion
  (102 shorter events, 13.5 us)
Async XLA Ops:
  0.6 3.5 %copy-start.3 = (f32[160,160,1]{1,0,2:T(8,128)S(1)}, f32[160,160,1]{1,0,2:T(8,128)}, u32[]{:S(2)}) copy-start(f32[160,160,1]{1,0,2:T(8,128)} %constant.105) | copy-start | bytes 307204
  3.8 1.4 copy-start.8
  5.2 1.8 %copy-start.10 = (f32[8,8,1]{1,0,2:T(8,128)S(1)}, f32[8,8,1]{1,0,2:T(8,128)}, u32[]{:S(2)}) copy-start(f32[8,8,1]{1,0,2:T(8,128)} %constant.107) | copy-start | bytes 772
  5.8 1.8 %copy-start.23 = (s32[48]{0:T(128)S(1)}, s32[48]{0:T(128)}, u32[]{:S(2)}) copy-start(s32[48]{0:T(128)} %param.36) | copy-start | bytes 580
  5.9 1.8 %copy-start.25 = (f32[48]{0:T(128)S(1)}, f32[48]{0:T(128)}, u32[]{:S(2)}) copy-start(f32[48]{0:T(128)} %param.35) | copy-start | bytes 580
  9.1 18.4 %copy-start.18 = (f32[1,3]{1,0:T(1,128)S(1)}, f32[1,3]{1,0:T(1,128)}, u32[]{:S(2)}) copy-start(f32[1,3]{1,0:T(1,128)} %param.33) | copy-start | bytes 40
  9.1 18.9 %copy-start.20 = (f32[8,8]{1,0:T(8,128)S(1)}, f32[8,8]{1,0:T(8,128)}, u32[]{:S(2)}) copy-start(f32[8,8]{1,0:T(8,128)} %constant.97.clone) | copy-start | bytes 772
  9.1 20.2 %copy-start.15 = (f32[1,8,8]{2,1,0:T(8,128)S(1)}, f32[1,8,8]{2,1,0:T(8,128)}, u32[]{:S(2)}) copy-start(f32[1,8,8]{2,1,0:T(8,128)} %constant.104) | copy-start | bytes 772
  10.6 31.0 %all-to-all-start = ((f32[64,1,800]{2,1,0:T(1,128)}), f32[64,1,800]{2,1,0:T(1,128)}, u32[]{:S(2)}, u32[]{:S(2)}) async-start(f32[64,1,800]{2,1,0:T(1,128)} %all_to_all.36), calls=%async_computation | async-start | bytes 458752 | tf_op jit(solution)/shard_map/all_to_all | solution.py:175
  28.7 0.6 copy-start.12
  30.7 1.7 %copy-start.26 = (s32[64]{0:T(128)S(1)}, s32[64]{0:T(128)}, u32[]{:S(2)}) copy-start(s32[64]{0:T(128)} %param.37) | copy-start | bytes 772
  36.0 1.1 copy-start
  38.5 9.6 %copy-start.19 = (f32[1,3]{1,0:T(1,128)S(1)}, f32[1,3]{1,0:T(1,128)}, u32[]{:S(2)}) copy-start(f32[1,3]{1,0:T(1,128)} %param.33) | copy-start | bytes 40
  38.5 10.2 %copy-start.14 = (pred[64,20]{1,0:T(8,128)(4,1)S(1)}, pred[64,20]{1,0:T(8,128)(4,1)}, u32[]{:S(2)}) copy-start(pred[64,20]{1,0:T(8,128)(4,1)} %compare_and_fusion) | copy-start | bytes 3844
  39.3 13.0 %copy-start.21 = (f32[8,100]{1,0:T(8,128)S(1)}, f32[8,100]{1,0:T(8,128)}, u32[]{:S(2)}) copy-start(f32[8,100]{1,0:T(8,128)} %param.38) | copy-start | bytes 9604
  39.3 13.0 %copy-start.22 = (f32[8,100]{1,0:T(8,128)S(1)}, f32[8,100]{1,0:T(8,128)}, u32[]{:S(2)}) copy-start(f32[8,100]{1,0:T(8,128)} %param.39) | copy-start | bytes 9604
  43.3 8.8 %all-to-all-start.1 = ((f32[8,1,800]{2,1,0:T(1,128)}), f32[8,1,800]{2,1,0:T(1,128)S(1)}, u32[]{:S(2)}, u32[]{:S(2)}) async-start(f32[8,1,800]{2,1,0:T(1,128)} %broadcast_in_dim.92), calls=%async_computation.1 | async-start | bytes 57344 | tf_op jit(solution)/shard_map/all_to_all | solution.py:175
  52.2 15.4 %copy-start.17 = (f32[8,100]{1,0:T(8,128)}, f32[8,100]{1,0:T(8,128)S(1)}, u32[]{:S(2)}) copy-start(f32[8,100]{1,0:T(8,128)S(1)} %reshape.288) | copy-start | bytes 9604
  53.2 25.6 %all-to-all-start.2 = ((f32[64,1,800]{2,1,0:T(1,128)}), f32[64,1,800]{2,1,0:T(1,128)}, u32[]{:S(2)}, u32[]{:S(2)}) async-start(f32[64,1,800]{2,1,0:T(1,128)} %broadcast_in_dim.100), calls=%async_computation.2 | async-start | bytes 458752 | tf_op jit(solution)/shard_map/all_to_all | solution.py:175
  67.7 13.2 %copy-start.11 = (f32[8,8,1]{1,0,2:T(8,128)S(1)}, f32[8,8,1]{1,0,2:T(8,128)}, u32[]{:S(2)}) copy-start(f32[8,8,1]{1,0,2:T(8,128)} %constant.107) | copy-start | bytes 772
  84.8 0.8 copy-start.9
  85.6 2.3 %copy-start.13 = (f32[1,8,8]{2,1,0:T(8,128)S(1)}, f32[1,8,8]{2,1,0:T(8,128)}, u32[]{:S(2)}) copy-start(f32[1,8,8]{2,1,0:T(8,128)} %copy-done.12) | copy-start | bytes 772
  85.6 2.3 %copy-start.16 = (f32[1,8,8]{2,1,0:T(8,128)S(1)}, f32[1,8,8]{2,1,0:T(8,128)}, u32[]{:S(2)}) copy-start(f32[1,8,8]{2,1,0:T(8,128)} %constant.104) | copy-start | bytes 772
  86.8 3.3 %copy-start.1 = (f32[2,1,8,80,160]{4,3,2,1,0:T(8,128)}, f32[2,1,8,80,160]{4,3,2,1,0:T(8,128)S(1)}, u32[]{:S(2)}) copy-start(f32[2,1,8,80,160]{4,3,2,1,0:T(8,128)S(1)} %convolution_bitcast_fusion.1) | copy-start | bytes 2457604
  96.7 2.5 %copy-start.2 = (f32[2,1,8,80,160]{4,3,2,1,0:T(8,128)S(1)}, f32[2,1,8,80,160]{4,3,2,1,0:T(8,128)}, u32[]{:S(2)}) copy-start(f32[2,1,8,80,160]{4,3,2,1,0:T(8,128)} %copy-done.1) | copy-start | bytes 2457604
  96.7 2.5 %copy-start.4 = (f32[8,80,80]{2,1,0:T(8,128)S(1)}, f32[8,80,80]{2,1,0:T(8,128)}, u32[]{:S(2)}) copy-start(f32[8,80,80]{2,1,0:T(8,128)} %get-tuple-element.5) | copy-start | bytes 614404
  96.7 2.5 %copy-start.6 = (f32[160,160]{1,0:T(8,128)S(1)}, f32[160,160]{1,0:T(8,128)}, u32[]{:S(2)}) copy-start(f32[160,160]{1,0:T(8,128)} %constant.92.clone) | copy-start | bytes 307204
  96.8 2.5 %copy-start.7 = (f32[160,160]{1,0:T(8,128)S(1)}, f32[160,160]{1,0:T(8,128)}, u32[]{:S(2)}) copy-start(f32[160,160]{1,0:T(8,128)} %constant.93.clone) | copy-start | bytes 307204
  105.4 0.9 copy-start.5
  106.4 6.4 %copy-start.27 = (s32[64]{0:T(128)S(1)}, s32[64]{0:T(128)}, u32[]{:S(2)}) copy-start(s32[64]{0:T(128)} %param.37) | copy-start | bytes 772
  106.4 30.1 %copy-start.24 = (s32[48]{0:T(128)S(1)}, s32[48]{0:T(128)}, u32[]{:S(2)}) copy-start(s32[48]{0:T(128)} %param.36) | copy-start | bytes 580
  108.1 28.3 %all-to-all-start.3 = ((f32[64,1,3200]{2,1,0:T(1,128)}), f32[64,1,3200]{2,1,0:T(1,128)S(1)}, u32[]{:S(2)}, u32[]{:S(2)}) async-start(f32[64,1,3200]{2,1,0:T(1,128)} %copy.152), calls=%async_computation.3 | async-start | bytes 1638400 | tf_op jit(solution)/shard_map/all_to_all | solution.py:175

commit v2 on v1

v2 whole, which is shorter than its diff:
```python
import math

import jax
import jax.numpy as jnp
import numpy as np
from jax import lax
from jax.experimental import pallas as pl
from jax.experimental.pallas import tpu as pltpu
from jax.sharding import Mesh
from jax.sharding import PartitionSpec as P

NX = 80
NY = 80
NZ = 8
ROWS = NZ * NY
LANES = 128
WIDE = 2 * LANES
SLAB = 100
GROUP = 64

magic_taps = (
    8.433424733352934e-07,
    -1.290557201342061e-05,
    8.76298447621056e-05,
    -0.00030158038132690465,
    0.001747237136729939,
    -0.009420470302010804,
    0.023738214637249424,
    0.0612625895831208,
    0.9940415697834004,
    -0.06048952891969835,
    -0.021030251609303816,
    0.013372634148547948,
    -0.0034412814449349387,
    0.0004944322768868992,
    -5.185986881173433e-05,
    2.7273449291197967e-06,
)
grid_step = 0.9
half_order = 14
spectrum_center = 13.0
spectrum_half = 17.0
exchange_coef = (3.0 / math.pi) ** (1.0 / 3.0)


def stencil_taps():
    factorial = math.factorial
    second_taps = {}
    first_taps = {}
    running = 0.0
    for offset in range(1, half_order + 1):
        weight_j = factorial(half_order) ** 2 / (
            factorial(half_order - offset) * factorial(half_order + offset)
        )
        tap_sign = (-1.0) ** (offset + 1)
        second_taps[offset] = 2.0 * tap_sign * weight_j / offset**2
        second_taps[-offset] = second_taps[offset]
        first_taps[offset] = tap_sign * weight_j / offset
        first_taps[-offset] = -first_taps[offset]
        running = running + 2.0 * second_taps[offset]
    second_taps[0] = -running
    return (second_taps, first_taps)


def band_matrix(length, taps):
    matrix = np.zeros((length, length))
    for offset, tap_value in taps.items():
        matrix = matrix + tap_value * np.eye(length, k=offset)
    return matrix


def axis_tables(length):
    second_taps, first_taps = stencil_taps()
    magic_band = band_matrix(
        length, {tap_index - 8: magic_taps[tap_index] for tap_index in range(16)}
    )
    return (
        band_matrix(length, second_taps) * (-0.5 / grid_step**2),
        band_matrix(length, first_taps) / grid_step,
        magic_band,
    )


def split_table(matrix):
    matrix = np.asarray(matrix, np.float32)
    high = matrix.astype(jnp.bfloat16)
    low = (matrix - high.astype(np.float32)).astype(jnp.bfloat16)
    return high, low


def lane_table(blocks):
    table = np.zeros((WIDE, WIDE))
    for (row, column), block in blocks.items():
        r, c = row * LANES, column * LANES
        table[r : r + NX, c : c + NX] = block
    return table


def tables():
    second_x, first_x, magic_x = axis_tables(NX)
    second_y, first_y, magic_y = axis_tables(NY)

    def packed(matrix):
        high, low = split_table(matrix)
        return np.concatenate([high, low, high], axis=1)

    return {
        "x_second": lane_table({(0, 0): second_x.T, (1, 1): second_x.T}).astype(np.float32),
        "x_first": lane_table({(1, 0): first_x.T, (0, 1): -first_x.T}).astype(np.float32),
        "x_magic": np.stack(split_table(lane_table({(0, 0): magic_x.T, (1, 1): magic_x.T}))),
        "x_magic_back": np.stack(split_table(lane_table({(0, 0): magic_x, (1, 1): magic_x}))),
        "y_all": packed(np.concatenate([magic_y, second_y, first_y], axis=0)),
        "y_back": packed(magic_y.T),
    }


def split(values):
    high = values.astype(jnp.bfloat16)
    low = (values - high.astype(jnp.float32)).astype(jnp.bfloat16)
    return high, low


def mul(left, right):
    return jnp.dot(left, right, preferred_element_type=jnp.float32)


def twist(values):
    return jnp.concatenate([values[:, LANES:], -values[:, :LANES]], axis=1)


def lanes_of(rows):
    return lax.broadcasted_iota(jnp.int32, (rows, LANES), 1)


def roll(values, shift):
    shift = shift % LANES
    return pltpu.roll(values, shift, 1) if shift else values


def compose(lane, parts):
    result = parts[-1][1]
    for end, values in reversed(parts[:-1]):
        result = jnp.where(lane < end, values, result)
    return result


def x_weights(vector_ref, second_ref, first_ref, weight_ref):
    qx, qy, qz = (vector_ref[0, d] for d in range(3))
    shift = 0.5 * (qx * qx + qy * qy + qz * qz)
    row = lax.broadcasted_iota(jnp.int32, (WIDE, WIDE), 0)
    column = lax.broadcasted_iota(jnp.int32, (WIDE, WIDE), 1)
    weights = second_ref[...] + qx * first_ref[...]
    weights = weights + jnp.where(row == column, shift, 0.0)
    high, low = split(weights)
    weight_ref[0] = high
    weight_ref[1] = low


def x_product(values, weight_ref):
    high, low = split(values)
    return mul(high, weight_ref[0]) + mul(high, weight_ref[1]) + mul(low, weight_ref[0])


def y_product(table_ref, values):
    high, low = split(values)
    return mul(table_ref[...], jnp.concatenate([high, high, low], axis=0))


CHUNK = 160


def forward_xy(vector_ref, field_ref, kinetic_ref, smooth_ref, y_all_ref, weight_ref, x_magic_ref):
    qy = vector_ref[0, 1]
    for z in range(NZ):
        rows = slice(z * NY, (z + 1) * NY)
        product = y_product(y_all_ref, field_ref[rows, :])
        smooth_ref[rows, :] = product[:NY]
        kinetic_ref[rows, :] = product[NY : 2 * NY] + twist(qy * product[2 * NY :])
    for start in range(0, ROWS, CHUNK):
        rows = slice(start, start + CHUNK)
        kinetic_ref[rows, :] += x_product(field_ref[rows, :], weight_ref)
        smooth_ref[rows, :] = x_product(smooth_ref[rows, :], x_magic_ref)


def z_sum(matrix, planes):
    results = []
    for v in range(NZ):
        total = None
        for z in range(NZ):
            if matrix[v, z] != 0.0:
                term = float(matrix[v, z]) * planes[z]
                total = term if total is None else total + term
        results.append(total)
    return results


def z_kinetic(vector_ref, field_ref, kinetic_ref, y):
    second_z, first_z, _ = axis_tables(NZ)
    qz = vector_ref[0, 2]
    planes = [field_ref[z * NY + y : z * NY + y + 8, :] for z in range(NZ)]
    turned = [qz * twist(p) for p in planes]
    for z, (a, b) in enumerate(zip(z_sum(second_z, planes), z_sum(first_z, turned))):
        kinetic_ref[z * NY + y : z * NY + y + 8, :] += a + b


def density_kernel(
    rank_ref,
    weight_k_ref,
    occupation_ref,
    slot_ref,
    vector_ref,
    linear_ref,
    second_ref,
    first_ref,
    x_magic_ref,
    y_all_ref,
    field_ref,
    kinetic_ref,
    smooth_ref,
    out_ref,
    parts_ref,
    weight_ref,
    rows_ref,
):
    x_weights(vector_ref, second_ref, first_ref, weight_ref)
    lane = lanes_of(ROWS // 4)
    tiles = [linear_ref[pl.ds(t, ROWS // 4, stride=5), :] for t in range(5)]
    for h in range(8):
        t, start = divmod(NX * h, LANES)
        base = tiles[t]
        if start + NX > LANES:
            base = jnp.where(lane >= start, base, tiles[t + 1])
        piece = jnp.where(lane < NX, roll(base, -start), 0.0)
        parts_ref[h % 2, pl.ds(h // 2, ROWS // 4, stride=4), :] = piece
    field_ref[:, :LANES] = parts_ref[0]
    field_ref[:, LANES:] = parts_ref[1]
    forward_xy(
        vector_ref, field_ref, kinetic_ref, smooth_ref, y_all_ref, weight_ref, x_magic_ref
    )
    scale = jnp.float32(0.0)
    for i in range(slot_ref.shape[0]):
        scale = scale + jnp.where(slot_ref[i] == rank_ref[0], occupation_ref[i], 0.0)
    scale = scale * weight_k_ref[0]
    magic_z = axis_tables(NZ)[2]
    for y in range(0, NY, 8):
        z_kinetic(vector_ref, field_ref, kinetic_ref, y)
        planes = [smooth_ref[z * NY + y : z * NY + y + 8, :] for z in range(NZ)]
        for z, plane in enumerate(z_sum(magic_z, planes)):
            smooth_ref[z * NY + y : z * NY + y + 8, :] = plane
            real, imaginary = plane[:, :LANES], plane[:, LANES:]
            rows_ref[z * NY + y : z * NY + y + 8, :] = scale * (
                real * real + imaginary * imaginary
            )
    groups = ROWS // 5
    lane = lanes_of(groups)
    rows = [rows_ref[pl.ds(t, groups, stride=5), :] for t in range(5)]
    for s in range(4):
        slab = jnp.where(
            lane < NX * (s + 1) - SLAB * s,
            roll(rows[s], NX * s - SLAB * s),
            roll(rows[s + 1], NX * (s + 1) - SLAB * s),
        )
        for z in range(NZ):
            out_ref[pl.ds(8 * s + z, 16, stride=32), :] = slab[16 * z : 16 * z + 16]


def total_kernel(in_ref, out_ref):
    total = in_ref[0]
    for i in range(1, in_ref.shape[0]):
        total = total + in_ref[i]
    for i in range(out_ref.shape[0]):
        out_ref[i] = total


def potential_kernel(in_ref, external_ref, core_ref, density_ref, out_ref, pad_ref):
    total = in_ref[0]
    for i in range(1, in_ref.shape[0]):
        total = total + in_ref[i]
    density = total[:, :SLAB]
    density_ref[...] = density
    root = jnp.exp(jnp.log(density + core_ref[...]) * (1.0 / 3.0))
    pad_ref[...] = jnp.zeros_like(pad_ref)
    pad_ref[:, :SLAB] = external_ref[...] - exchange_coef * root
    padded = pad_ref[...]
    for i in range(out_ref.shape[0]):
        out_ref[i] = padded


def filter_kernel(
    count_ref,
    vector_ref,
    field_ref,
    kinetic_ref,
    smooth_ref,
    slabs_ref,
    second_ref,
    first_ref,
    x_magic_ref,
    x_back_ref,
    y_all_ref,
    y_back_ref,
    out_ref,
    potential_ref,
    weight_ref,
    term_ref,
    wave_ref,
    kin_ref,
    work_ref,
    parts_ref,
    owned_ref,
):
    x_weights(vector_ref, second_ref, first_ref, weight_ref)
    lane = lanes_of(16)
    for z in range(NZ):
        slabs = [slabs_ref[pl.ds(8 * s + z, 16, stride=32), :] for s in range(4)]
        for t in range(5):
            if t == 0:
                row = slabs[0]
            elif t == 4:
                row = roll(slabs[3], SLAB * 3 - NX * 4)
            else:
                row = jnp.where(
                    lane < SLAB * t - NX * t,
                    roll(slabs[t - 1], SLAB * (t - 1) - NX * t),
                    roll(slabs[t], SLAB * t - NX * t),
                )
            potential_ref[pl.ds(z * NY + t, 16, stride=5), :] = row
    magic_z = axis_tables(NZ)[2]

    def weighted(planes, y):
        result = []
        for z, plane in enumerate(planes):
            potential = potential_ref[z * NY + y : z * NY + y + 8, :]
            result.append(plane * jnp.concatenate([potential, potential], axis=1))
        return result

    def backward(values_ref):
        for z in range(NZ):
            rows = slice(z * NY, (z + 1) * NY)
            values_ref[rows, :] = y_product(y_back_ref, values_ref[rows, :])

    for y in range(0, NY, 8):
        planes = [smooth_ref[z * NY + y : z * NY + y + 8, :] for z in range(NZ)]
        for z, plane in enumerate(z_sum(magic_z.T, weighted(planes, y))):
            work_ref[z * NY + y : z * NY + y + 8, :] = plane
    backward(work_ref)
    for start in range(0, ROWS, CHUNK):
        rows = slice(start, start + CHUNK)
        applied = kinetic_ref[rows, :] + x_product(work_ref[rows, :], x_back_ref)
        term_ref[rows, :] = (applied - spectrum_center * field_ref[rows, :]) * (
            1.0 / spectrum_half
        )
    forward_xy(vector_ref, term_ref, kin_ref, wave_ref, y_all_ref, weight_ref, x_magic_ref)
    for y in range(0, NY, 8):
        z_kinetic(vector_ref, term_ref, kin_ref, y)
        planes = [wave_ref[z * NY + y : z * NY + y + 8, :] for z in range(NZ)]
        planes = weighted(z_sum(magic_z, planes), y)
        for z, plane in enumerate(z_sum(magic_z.T, planes)):
            work_ref[z * NY + y : z * NY + y + 8, :] = plane
    backward(work_ref)
    for start in range(0, ROWS, CHUNK):
        rows = slice(start, start + CHUNK)
        image = kin_ref[rows, :] + x_product(work_ref[rows, :], x_back_ref)
        image = image - spectrum_center * term_ref[rows, :]
        filtered = (2.0 / spectrum_half) * image - field_ref[rows, :]
        parts_ref[0, rows, :] = filtered[:, :LANES]
        parts_ref[1, rows, :] = filtered[:, LANES:]
    parts_ref[:, ROWS:, :] = jnp.zeros((2, parts_ref.shape[1] - ROWS, LANES), jnp.float32)
    offset = 0
    for d in range(GROUP):
        for part in range(2):
            owned_ref[part, 24 * d : 24 * d + 24, :] = parts_ref[part, pl.ds(offset, 24), :]
        offset = offset + count_ref[d]
    lane = lanes_of(GROUP)
    for q in range(5):
        pieces = [
            roll(owned_ref[h % 2, pl.ds(4 * q + h // 2, GROUP, stride=24), :], NX * h)
            for h in range(8)
        ]
        for t in range(5):
            first, last = LANES * t // NX, (LANES * t + LANES - 1) // NX
            parts = [(NX * (h + 1) - LANES * t, pieces[h]) for h in range(first, last + 1)]
            out_ref[pl.ds(5 * q + t, GROUP, stride=25), :] = compose(lane, parts)


def gram_kernel(rank_ref, count_ref, slot_ref, in_ref, stack_ref, out_ref, chosen_ref):
    orbitals = slot_ref.shape[0]
    for i in range(orbitals):
        chosen_ref[pl.ds(i, 25, stride=orbitals), :] = in_ref[pl.ds(25 * slot_ref[i], 25), :]
    limit = 2 * NX * count_ref[rank_ref[0]]
    lane = lanes_of(orbitals)
    total = jnp.zeros((2 * orbitals, WIDE), jnp.float32)
    empty = jnp.zeros((64 - orbitals, LANES), jnp.bfloat16)
    for q in range(5):
        tiles = []
        for t in range(5):
            place = 5 * q + t
            tile = chosen_ref[place * orbitals : (place + 1) * orbitals, :]
            tiles.append(jnp.where(lane < limit - LANES * place, tile, 0.0))
        ahead = [roll(tile, -NX) for tile in tiles]
        behind = [roll(tile, NX) for tile in tiles]
        lefts, rights = [], []
        for t in range(5):
            parts, position = [], LANES * t
            while position < LANES * (t + 1):
                h = position // NX
                shift = NX if h % 2 == 0 else -NX
                source = (position + shift) // LANES
                end = min(
                    NX * (h + 1), LANES * (source + 1) - shift, LANES * (t + 1)
                )
                values = ahead[source] if h % 2 == 0 else -behind[source]
                parts.append((end - LANES * t, values))
                position = end
            turned = compose(lane, parts)
            high, low = split(tiles[t])
            turned_high, turned_low = split(turned)
            right = jnp.concatenate(
                [high, empty, turned_high, empty, low, empty, turned_low, empty], axis=0
            )
            stack_ref[5 * q + t] = right
            lefts.append(jnp.concatenate([high, low], axis=0))
            rights.append(right)
        total = total + lax.dot_general(
            jnp.concatenate(lefts, axis=1),
            jnp.concatenate(rights, axis=1),
            (((1,), (1,)), ((), ())),
            preferred_element_type=jnp.float32,
        )
    both = total[:orbitals, :LANES] + (
        total[orbitals:, :LANES] + total[:orbitals, LANES:]
    )
    row = lax.broadcasted_iota(jnp.int32, (orbitals, LANES), 0)
    packed = jnp.where(row <= lane, both, roll(both, 64))
    half = orbitals // 2
    lane = lanes_of(half)
    folded = jnp.where(lane < 64, packed[:half], roll(packed[half:], 64))
    for i in range(out_ref.shape[0]):
        out_ref[i] = folded


def rotate_kernel(in_ref, stack_ref, out_ref):
    orbitals = out_ref.shape[0]
    folded = in_ref[0]
    for i in range(1, in_ref.shape[0]):
        folded = folded + in_ref[i]
    lane = lanes_of(orbitals)
    row = lax.broadcasted_iota(jnp.int32, (orbitals, LANES), 0)
    packed = jnp.concatenate([folded, roll(folded, 64)], axis=0)
    packed = jnp.where(lane < orbitals, packed, 0.0)
    square = jnp.concatenate(
        [packed, jnp.zeros((LANES - orbitals, LANES), jnp.float32)], axis=0
    )
    flipped = square.T[:orbitals]
    real = jnp.where(row <= lane, packed, flipped)
    imaginary = jnp.where(row < lane, -flipped, jnp.where(row > lane, packed, 0.0))
    diagonal = row == lane
    components = ROWS * 2 * NX
    trace = jnp.sum(jnp.where(diagonal, real, 0.0), keepdims=True)
    mean_square = trace / (orbitals * components) + 1e-06
    shrink = 0.5 / (components * mean_square)
    inverse = 1.0 / jnp.sqrt(mean_square)
    inside = lane < orbitals
    over_self = jnp.where(diagonal, 1.5, 0.0) - shrink * real
    over_turned = -shrink * imaginary
    left = jnp.where(inside, over_self, 0.0) + roll(jnp.where(inside, over_turned, 0.0), 64)
    high, low = split(left * inverse)
    left = jnp.concatenate(
        [
            jnp.concatenate([high, high], axis=1),
            jnp.concatenate([low, jnp.zeros_like(low)], axis=1),
        ],
        axis=0,
    )
    for q in range(5):
        right = jnp.concatenate([stack_ref[5 * q + t] for t in range(5)], axis=1)
        both = mul(left, right)
        out_ref[:, 640 * q : 640 * (q + 1)] = both[:orbitals] + both[orbitals:]


def shaped(shape, dtype=jnp.float32):
    return jax.ShapeDtypeStruct(shape, dtype)


def call(body, kinds, outs, scratch=(), limit=48):
    spaces = {"s": pltpu.SMEM, "v": pltpu.VMEM}
    many = isinstance(outs, (list, tuple))
    one = pl.BlockSpec(memory_space=pltpu.VMEM)
    return pl.pallas_call(
        body,
        out_shape=outs,
        in_specs=[pl.BlockSpec(memory_space=spaces[k]) for k in kinds],
        out_specs=(one,) * len(outs) if many else one,
        scratch_shapes=list(scratch),
        compiler_params=pltpu.CompilerParams(vmem_limit_bytes=limit << 20),
    )


def field_scratch():
    return pltpu.VMEM((ROWS, WIDE), jnp.float32)


def run_density(rank, weight, occupation, slots, vector, linear, table):
    field = shaped((ROWS, WIDE))
    return call(
        density_kernel,
        "sssssvvvvv",
        (field, field, field, shaped((GROUP * NZ, LANES))),
        (
            pltpu.VMEM((2, ROWS, LANES), jnp.float32),
            pltpu.VMEM((2, WIDE, WIDE), jnp.bfloat16),
            pltpu.VMEM((ROWS, LANES), jnp.float32),
        ),
    )(
        rank, weight, occupation, slots, vector, linear,
        table["x_second"], table["x_first"], table["x_magic"], table["y_all"],
    )


def run_total(values, count):
    return call(total_kernel, "v", shaped((count,) + values.shape[1:]))(values)


def run_potential(values, external, core):
    return call(
        potential_kernel,
        "vvv",
        (shaped(external.shape), shaped((GROUP, NZ, LANES))),
        (pltpu.VMEM((NZ, LANES), jnp.float32),),
    )(values, external, core)


def run_filter(counts, vector, field, kinetic, smooth, slabs, table):
    return call(
        filter_kernel,
        "ssvvvvvvvvvv",
        shaped((GROUP * 25, LANES)),
        (
            pltpu.VMEM((ROWS, LANES), jnp.float32),
            pltpu.VMEM((2, WIDE, WIDE), jnp.bfloat16),
            field_scratch(),
            field_scratch(),
            field_scratch(),
            field_scratch(),
            pltpu.VMEM((2, ROWS + 24, LANES), jnp.float32),
            pltpu.VMEM((2, GROUP * 24, LANES), jnp.float32),
        ),
    )(
        counts, vector, field, kinetic, smooth, slabs,
        table["x_second"], table["x_first"], table["x_magic"], table["x_magic_back"],
        table["y_all"], table["y_back"],
    )


def run_gram(rank, counts, slots, received):
    orbitals = slots.shape[0]
    return call(
        gram_kernel,
        "sssv",
        (shaped((25, WIDE, LANES), jnp.bfloat16), shaped((8, orbitals // 2, LANES))),
        (pltpu.VMEM((25 * orbitals, LANES), jnp.float32),),
    )(rank, counts, slots, received)


def run_rotate(values, stack, orbitals):
    return call(rotate_kernel, "vv", shaped((orbitals, 25 * LANES)))(values, stack)


def exchange(values, axes):
    return lax.all_to_all(values, axes, split_axis=0, concat_axis=0, tiled=True)


def on_device(
    wavefunctions,
    kpoint_vector,
    kpoint_weight,
    occupation,
    orbital_slot,
    piece_rows,
    external_potential,
    core_density,
):
    kpt, orb = ("kpt",), ("orb_y", "orb_z")
    rank = lax.axis_index(orb).astype(jnp.int32).reshape(1)
    table = {name: jnp.asarray(value) for name, value in tables().items()}
    field, kinetic, smooth, partial_density = run_density(
        rank, kpoint_weight, occupation, orbital_slot, kpoint_vector,
        wavefunctions.reshape(-1, LANES), table,
    )
    terms = exchange(partial_density.reshape(GROUP, NZ, LANES), orb)
    terms = exchange(run_total(terms, 8), kpt)
    density, slabs = run_potential(terms, external_potential, core_density)
    slabs = exchange(slabs, orb).reshape(GROUP * NZ, LANES)
    outgoing = run_filter(piece_rows, kpoint_vector, field, kinetic, smooth, slabs, table)
    received = exchange(outgoing.reshape(GROUP, 25 * LANES), orb).reshape(GROUP * 25, LANES)
    stack, packed = run_gram(rank, piece_rows, orbital_slot, received)
    packed = exchange(packed, ("orb_z",))
    packed = exchange(run_total(packed, 8), ("orb_y",))
    return (density, run_rotate(packed, stack, orbital_slot.shape[0])[None])


def solution(mesh):
    side = math.isqrt(mesh.shape["orb"])
    fine = Mesh(
        mesh.devices.reshape(mesh.shape["kpt"], -1, side), ("kpt", "orb_y", "orb_z")
    )
    orb = ("orb_y", "orb_z")
    in_specs = (
        P("kpt", orb, None),
        P("kpt", None),
        P("kpt"),
        P(),
        P(),
        P(),
        P(None, orb),
        P(None, orb),
    )
    out_specs = (P(None, orb), P("kpt", None, orb))
    return jax.shard_map(
        on_device, mesh=fine, in_specs=in_specs, out_specs=out_specs, check_vma=False
    )
```

time: 169 us -> 132 us (0.78)
  blocking collectives: 24.1 us -> 112 us
  starting transfers between devices: 38 us -> 0 us
  waiting for transfers between devices: 35.9 us -> 0 us
  matrix products: 28.4 us -> 0 us
  local copies, waits for them, and re-layouts: 22.1 us -> 6.75 us
  other arithmetic: 15.1 us -> 0 us
  Pallas kernels: 0 us -> 12.1 us
  between operations: 4.05 us -> 1.41 us
    all_to_all x2 -> x6, blocking collectives: 24.1 us -> 112 us  [exchange(): return lax.all_to_all(values, axes, split_axis=0, concat_axis=0, tiled=True)]
    all_to_all x4 -> x0, starting transfers between devices: 38 us -> none  [exchange(): return lax.all_to_all(values, axes, split_axis=0, concat_axis=0, tiled=True)]
    all_to_all x4 -> x0, waiting for transfers between devices: 35.9 us -> none  [exchange(): return lax.all_to_all(values, axes, split_axis=0, concat_axis=0, tiled=True)]
    dot_general x21 -> x0, matrix products: 28.4 us -> none  [the longest x6 9.32 us: apply_last(): return jnp.einsum('azyc,dc->azyd', grid_field, matrix, precision=exact_mode)]
    pallas_call x0 -> x7, Pallas kernels: none -> 12.1 us  [the longest x1 5.13 us: run_filter(): call(filter_kernel, 'ssvvvvvvvvvv', shaped((GROUP * 25, LANES)), (pltpu.V...]
    gather x2 -> x0, local copies, waits for them, and re-layouts: 3.95 us -> none  [on_device(): jnp.take(filtered_rows, positions, axis=0)]
    reduce_sum x9 -> x0, other arithmetic: 3.82 us -> none  [the longest x1 1.11 us: on_device(): own_density = jnp.sum(exchange(by_owner, orb), axis=0)]
    unnamed x57 -> x34, local copies, waits for them, and re-layouts: 3.11 us -> 6.75 us
  transfers between devices with their start and end apart: 4 -> 0, of which waited for: 4 -> 0; matrix products, arithmetic and copies ran while one was open for 10% -> 0% of each run, Pallas kernels for 0% -> 0%
where the time goes in v2:
time: 132 us
  blocking collectives  112 us (85%)
  Pallas kernels  12.1 us (9%)
  local copies, waits for them, and re-layouts  6.75 us (5%)
  between operations  1.41 us (1%)
    all_to_all x6, blocking collectives, exchange(): return lax.all_to_all(values, axes, split_axis=0, concat_axis=0, tiled=True)  112 us
    unnamed x34, local copies, waits for them, and re-layouts  6.75 us
    pallas_call x1, Pallas kernels, run_filter(): call(filter_kernel, 'ssvvvvvvvvvv', shaped((GROUP * 25, LANES)), (pltpu.V...  5.13 us
    pallas_call x1, Pallas kernels, run_density(): call(density_kernel, 'sssssvvvvv', (field, field, field, shaped((GROUP *...  2.92 us

profile of v2, /device:TPU:2, one launch (start us, length us, event | category | flops | bytes accessed | tf_op | source)
XLA Modules:
  0.0 132.0 jit_solution(16276392146875646764)
XLA Ops:
  0.6 0.0 copy-start.12
  0.6 0.0 copy-start.10
  0.7 0.0 copy-start.9
  0.7 0.0 copy-start.15
  1.3 0.0 copy-start
  1.3 0.9 copy-done
  2.3 0.0 copy-start.2
  2.3 0.9 copy-done.2
  3.2 0.0 copy-start.4
  3.2 0.9 copy-done.4
  4.2 0.0 copy-start.5
  4.2 0.9 copy-done.5
  5.1 0.0 copy-start.6
  5.1 1.0 copy-done.6
  6.1 0.0 copy-start.11
  6.1 0.7 copy-done.11
  6.7 0.0 copy-start.13
  6.8 0.7 copy-done.13
  7.4 0.0 copy-start.16
  7.4 0.7 copy-done.16
  8.1 0.0 copy-start.1
  8.1 0.0 copy-start.3
  8.1 0.0 copy-start.7
  8.1 0.0 copy-start.8
  8.1 2.9 %shard_map.149 = (f32[640,256]{1,0:T(8,128)S(1)}, f32[640,256]{1,0:T(8,128)S(1)}, f32[640,256]{1,0:T(8,128)S(1)}, f32[512,128]{1,0:T(8,128)S(1)}) custom-call(s32[1]{0:T(128)} %bitcast.rank_ref, f32[1]{0:T(128)S(6)} %copy.17.weight_k_ref, f32[48]{0:T(128)S(1)} %copy-done.16, s32[48]{0:T(128)S(1)} %copy-done.13, f32[1,3]{1,0:T(1,128)S(1)} %copy-done.11, ...), custom_call_target="tpu_custom_call" | custom-call | tf_op jit(solution)/shard_map/pallas_call | solution.py:505
  11.0 31.4 %all_to_all.34.in_ref = f32[64,8,128]{2,1,0:T(8,128)S(1)} all-to-all(f32[64,8,128]{2,1,0:T(8,128)S(1)} %bitcast.11), channel_id=1, replica_groups=mesh['kpt'=8,'orb_y'=8,'orb_z'=8] {'orb_y','orb_z'}, dimensions={0} | all-to-all | bytes 524288 | tf_op jit(solution)/shard_map/all_to_all | solution.py:570
  42.4 0.1 shard_map.150
  42.4 8.6 %all_to_all.35.in_ref = f32[8,8,128]{2,1,0:T(8,128)S(1)} all-to-all(f32[8,8,128]{2,1,0:T(8,128)S(1)} %shard_map.150), channel_id=1, replica_groups=mesh['kpt'=8,'orb_y'=8,'orb_z'=8] {'kpt'}, dimensions={0} | all-to-all | bytes 65536 | tf_op jit(solution)/shard_map/all_to_all | solution.py:570
  51.1 0.0 copy-done.10
  51.1 0.0 copy-done.9
  51.1 0.6 shard_map.151
  51.7 19.0 %all_to_all.36 = f32[64,8,128]{2,1,0:T(8,128)S(1)} all-to-all(f32[64,8,128]{2,1,0:T(8,128)S(1)} %get-tuple-element.15), channel_id=1, replica_groups=mesh['kpt'=8,'orb_y'=8,'orb_z'=8] {'orb_y','orb_z'}, dimensions={0} | all-to-all | bytes 524288 | tf_op jit(solution)/shard_map/all_to_all | solution.py:570
  70.7 0.0 copy-done.12
  70.7 0.0 copy-done.15
  70.7 0.0 copy-done.1
  70.7 0.0 copy-done.3
  70.7 0.0 copy-done.7
  70.7 0.0 copy-done.8
  70.8 5.1 %shard_map.152 = f32[1600,128]{1,0:T(8,128)S(1)} custom-call(s32[64]{0:T(128)S(1)} %copy-done.15, f32[1,3]{1,0:T(1,128)S(1)} %copy-done.12, f32[640,256]{1,0:T(8,128)S(1)} %get-tuple-element.12.field_ref, f32[640,256]{1,0:T(8,128)S(1)} %get-tuple-element.13.kinetic_ref, f32[640,256]{1,0:T(8,128)S(1)} %get-tuple-element.14.smooth_ref, ...), custom_call_target="tpu_custom_call" | custom-call | tf_op jit(solution)/shard_map/pallas_call | solution.py:534
  75.9 0.0 copy-start.14
  75.9 28.0 %all_to_all.37 = f32[64,1,3200]{2,1,0:T(1,128)S(1)} all-to-all(f32[64,1,3200]{2,1,0:T(1,128)S(1)} %bitcast.8), channel_id=1, replica_groups=mesh['kpt'=8,'orb_y'=8,'orb_z'=8] {'orb_y','orb_z'}, dimensions={0} | all-to-all | bytes 1638400 | tf_op jit(solution)/shard_map/all_to_all | solution.py:570
  103.9 0.0 copy-done.14
  103.9 1.8 %shard_map.153 = (bf16[25,256,128]{2,1,0:T(8,128)(2,1)S(1)}, f32[8,24,128]{2,1,0:T(8,128)S(1)}) custom-call(s32[1]{0:T(128)} %bitcast.rank_ref, s32[64]{0:T(128)S(1)} %copy-done.15, s32[48]{0:T(128)S(1)} %copy-done.14, f32[1600,128]{1,0:T(8,128)S(1)} %bitcast.7), custom_call_target="tpu_custom_call" | custom-call | tf_op jit(solution)/shard_map/pallas_call | solution.py:557
  105.7 13.6 %all_to_all.38.in_ref = f32[8,24,128]{2,1,0:T(8,128)S(1)} all-to-all(f32[8,24,128]{2,1,0:T(8,128)S(1)} %get-tuple-element.16), channel_id=1, replica_groups=mesh['kpt'=8,'orb_y'=8,'orb_z'=8] {'orb_z'}, dimensions={0} | all-to-all | bytes 196608 | tf_op jit(solution)/shard_map/all_to_all | solution.py:570
  119.3 11.1 %all_to_all.39.in_ref = f32[8,24,128]{2,1,0:T(8,128)S(1)} all-to-all(f32[8,24,128]{2,1,0:T(8,128)S(1)} %shard_map.154), channel_id=1, replica_groups=mesh['kpt'=8,'orb_y'=8,'orb_z'=8] {'orb_y'}, dimensions={0} | all-to-all | bytes 196608 | tf_op jit(solution)/shard_map/all_to_all | solution.py:570
  130.4 1.6 %shard_map.155 = f32[48,3200]{1,0:T(8,128)} custom-call(f32[8,24,128]{2,1,0:T(8,128)S(1)} %all_to_all.39.in_ref, bf16[25,256,128]{2,1,0:T(8,128)(2,1)S(1)} %get-tuple-element.17.stack_ref), custom_call_target="tpu_custom_call" | custom-call | tf_op jit(solution)/shard_map/pallas_call | solution.py:566
  (1 shorter events, 0.0 us)
Async XLA Ops:
  0.6 70.1 %copy-start.12 = (f32[1,3]{1,0:T(1,128)S(1)}, f32[1,3]{1,0:T(1,128)}, u32[]{:S(2)}) copy-start(f32[1,3]{1,0:T(1,128)} %vector_ref.3) | copy-start | bytes 40
  0.6 50.4 %copy-start.10 = (f32[8,100]{1,0:T(8,128)S(1)}, f32[8,100]{1,0:T(8,128)}, u32[]{:S(2)}) copy-start(f32[8,100]{1,0:T(8,128)} %core_ref.1) | copy-start | bytes 9604
  0.7 50.4 %copy-start.9 = (f32[8,100]{1,0:T(8,128)S(1)}, f32[8,100]{1,0:T(8,128)}, u32[]{:S(2)}) copy-start(f32[8,100]{1,0:T(8,128)} %external_ref.1) | copy-start | bytes 9604
  0.7 70.1 %copy-start.15 = (s32[64]{0:T(128)S(1)}, s32[64]{0:T(128)}, u32[]{:S(2)}) copy-start(s32[64]{0:T(128)} %count_ref.3) | copy-start | bytes 772
  1.3 1.0 copy-start
  2.3 0.9 copy-start.2
  3.2 0.9 copy-start.4
  4.2 0.9 copy-start.5
  5.1 1.0 copy-start.6
  6.1 0.7 copy-start.11
  6.7 0.7 copy-start.13
  7.4 0.7 copy-start.16
  8.1 62.7 %copy-start.1 = (bf16[2,256,256]{2,1,0:T(8,128)(2,1)S(1)}, bf16[2,256,256]{2,1,0:T(8,128)(2,1)}, u32[]{:S(2)}) copy-start(bf16[2,256,256]{2,1,0:T(8,128)(2,1)} %constant.23.clone.x_magic_ref) | copy-start | bytes 786436
  8.1 62.7 %copy-start.3 = (f32[256,256]{1,0:T(8,128)S(1)}, f32[256,256]{1,0:T(8,128)}, u32[]{:S(2)}) copy-start(f32[256,256]{1,0:T(8,128)} %constant.22.clone.first_ref) | copy-start | bytes 786436
  8.1 62.7 %copy-start.7 = (bf16[2,256,256]{2,1,0:T(8,128)(2,1)S(1)}, bf16[2,256,256]{2,1,0:T(8,128)(2,1)}, u32[]{:S(2)}) copy-start(bf16[2,256,256]{2,1,0:T(8,128)(2,1)} %constant.24.clone.x_back_ref) | copy-start | bytes 786436
  8.1 62.7 %copy-start.8 = (bf16[80,240]{1,0:T(8,128)(2,1)S(1)}, bf16[80,240]{1,0:T(8,128)(2,1)}, u32[]{:S(2)}) copy-start(bf16[80,240]{1,0:T(8,128)(2,1)} %constant.26.clone.y_back_ref) | copy-start | bytes 115204
  75.9 28.0 %copy-start.14 = (s32[48]{0:T(128)S(1)}, s32[48]{0:T(128)}, u32[]{:S(2)}) copy-start(s32[48]{0:T(128)} %slot_ref.3) | copy-start | bytes 580

commit v3 on v2

--- a/solution.py
+++ b/solution.py
@@ -1,3 +1,4 @@
+import functools
 import math
 
 import jax
@@ -88,11 +89,9 @@
     return high, low
 
 
-def lane_table(blocks):
-    table = np.zeros((WIDE, WIDE))
-    for (row, column), block in blocks.items():
-        r, c = row * LANES, column * LANES
-        table[r : r + NX, c : c + NX] = block
+def padded(block):
+    table = np.zeros((LANES, LANES))
+    table[:NX, :NX] = block
     return table
 
 
@@ -105,10 +104,9 @@
         return np.concatenate([high, low, high], axis=1)
 
     return {
-        "x_second": lane_table({(0, 0): second_x.T, (1, 1): second_x.T}).astype(np.float32),
-        "x_first": lane_table({(1, 0): first_x.T, (0, 1): -first_x.T}).astype(np.float32),
-        "x_magic": np.stack(split_table(lane_table({(0, 0): magic_x.T, (1, 1): magic_x.T}))),
-        "x_magic_back": np.stack(split_table(lane_table({(0, 0): magic_x, (1, 1): magic_x}))),
+        "x_kinetic": np.stack([padded(second_x.T), padded(first_x.T)]).astype(np.float32),
+        "x_magic": np.stack(split_table(padded(magic_x.T))),
+        "x_back": np.stack(split_table(padded(magic_x))),
         "y_all": packed(np.concatenate([magic_y, second_y, first_y], axis=0)),
         "y_back": packed(magic_y.T),
     }
@@ -144,16 +142,25 @@
     return result
 
 
-def x_weights(vector_ref, second_ref, first_ref, weight_ref):
+def both_halves(table):
+    zero = jnp.zeros_like(table)
+    return jnp.concatenate(
+        [jnp.concatenate([table, zero], axis=1), jnp.concatenate([zero, table], axis=1)], axis=0
+    )
+
+
+def x_weights(vector_ref, table_ref, weight_ref):
     qx, qy, qz = (vector_ref[0, d] for d in range(3))
     shift = 0.5 * (qx * qx + qy * qy + qz * qz)
-    row = lax.broadcasted_iota(jnp.int32, (WIDE, WIDE), 0)
-    column = lax.broadcasted_iota(jnp.int32, (WIDE, WIDE), 1)
-    weights = second_ref[...] + qx * first_ref[...]
-    weights = weights + jnp.where(row == column, shift, 0.0)
-    high, low = split(weights)
-    weight_ref[0] = high
-    weight_ref[1] = low
+    row = lax.broadcasted_iota(jnp.int32, (LANES, LANES), 0)
+    column = lax.broadcasted_iota(jnp.int32, (LANES, LANES), 1)
+    same_high, same_low = split(table_ref[0] + jnp.where(row == column, shift, 0.0))
+    cross_high, cross_low = split(qx * table_ref[1])
+    for i, (same, cross) in enumerate([(same_high, cross_high), (same_low, cross_low)]):
+        weight_ref[i, :LANES, :LANES] = same
+        weight_ref[i, LANES:, LANES:] = same
+        weight_ref[i, LANES:, :LANES] = cross
+        weight_ref[i, :LANES, LANES:] = -cross
 
 
 def x_product(values, weight_ref):
@@ -204,25 +211,56 @@
 
 
 def density_kernel(
-    rank_ref,
+    axes,
+    weight_k_hbm,
+    occupation_hbm,
+    slot_hbm,
+    vector_hbm,
+    linear_hbm,
+    x_kinetic_hbm,
+    x_magic_hbm,
+    y_all_hbm,
+    field_ref,
+    kinetic_ref,
+    smooth_ref,
+    weight_ref,
+    out_ref,
     weight_k_ref,
     occupation_ref,
     slot_ref,
     vector_ref,
     linear_ref,
-    second_ref,
-    first_ref,
+    x_kinetic_ref,
+    x_half_ref,
+    y_all_ref,
+    parts_ref,
     x_magic_ref,
-    y_all_ref,
-    field_ref,
-    kinetic_ref,
-    smooth_ref,
-    out_ref,
-    parts_ref,
-    weight_ref,
     rows_ref,
+    arrived,
 ):
-    x_weights(vector_ref, second_ref, first_ref, weight_ref)
+    copies = [
+        pltpu.make_async_copy(source, target, arrived.at[i])
+        for i, (source, target) in enumerate(
+            [
+                (linear_hbm, linear_ref),
+                (vector_hbm, vector_ref),
+                (x_kinetic_hbm, x_kinetic_ref),
+                (x_magic_hbm, x_half_ref),
+                (y_all_hbm, y_all_ref),
+                (weight_k_hbm, weight_k_ref),
+                (occupation_hbm, occupation_ref),
+                (slot_hbm, slot_ref),
+            ]
+        )
+    ]
+    for copy in copies:
+        copy.start()
+    for copy in copies:
+        copy.wait()
+    rank = lax.axis_index(axes) if axes else 0
+    x_weights(vector_ref, x_kinetic_ref, weight_ref)
+    for i in range(2):
+        x_magic_ref[i] = both_halves(x_half_ref[i])
     lane = lanes_of(ROWS // 4)
     tiles = [linear_ref[pl.ds(t, ROWS // 4, stride=5), :] for t in range(5)]
     for h in range(8):
@@ -239,7 +277,7 @@
     )
     scale = jnp.float32(0.0)
     for i in range(slot_ref.shape[0]):
-        scale = scale + jnp.where(slot_ref[i] == rank_ref[0], occupation_ref[i], 0.0)
+        scale = scale + jnp.where(slot_ref[i] == rank, occupation_ref[i], 0.0)
     scale = scale * weight_k_ref[0]
     magic_z = axis_tables(NZ)[2]
     for y in range(0, NY, 8):
@@ -260,8 +298,24 @@
             roll(rows[s], NX * s - SLAB * s),
             roll(rows[s + 1], NX * (s + 1) - SLAB * s),
         )
-        for z in range(NZ):
-            out_ref[pl.ds(8 * s + z, 16, stride=32), :] = slab[16 * z : 16 * z + 16]
+        last = slab[16 * (NZ - 1) :]
+        for z in range(NZ - 1):
+            tile = slab[16 * z : 16 * z + 16]
+            if z < 4:
+                tile = jnp.where(lane[:16] < SLAB, tile, roll(last, SLAB - 25 * z))
+            out_ref[pl.ds(7 * s + z, 16, stride=28), :] = tile
+
+
+def first_total_kernel(in_ref, out_ref):
+    total = in_ref[:56, :]
+    for i in range(1, GROUP // 8):
+        total = total + in_ref[56 * i : 56 * (i + 1), :]
+    rows = total[:7]
+    for i in range(1, 8):
+        rows = rows + total[7 * i : 7 * (i + 1)]
+    for i in range(out_ref.shape[0]):
+        out_ref[i, :7, :] = rows
+        out_ref[i, 7:, :] = jnp.zeros((1, LANES), jnp.float32)
 
 
 def total_kernel(in_ref, out_ref):
@@ -272,18 +326,32 @@
         out_ref[i] = total
 
 
-def potential_kernel(in_ref, external_ref, core_ref, density_ref, out_ref, pad_ref):
+def last_plane(lane, rows):
+    return compose(lane, [(25 * (c + 1), roll(rows[c], 25 * c - SLAB)) for c in range(4)])
+
+
+def potential_kernel(in_ref, external_ref, core_ref, density_ref, out_ref, pad_ref, many_ref):
     total = in_ref[0]
     for i in range(1, in_ref.shape[0]):
         total = total + in_ref[i]
-    density = total[:, :SLAB]
+    pad_ref[...] = total
+    one = lanes_of(1)
+    pad_ref[7:, :] = last_plane(one, [total[c : c + 1] for c in range(4)])
+    density = pad_ref[:, :SLAB]
     density_ref[...] = density
     root = jnp.exp(jnp.log(density + core_ref[...]) * (1.0 / 3.0))
-    pad_ref[...] = jnp.zeros_like(pad_ref)
+    pad_ref[:, SLAB:] = jnp.zeros((NZ, LANES - SLAB), jnp.float32)
     pad_ref[:, :SLAB] = external_ref[...] - exchange_coef * root
-    padded = pad_ref[...]
-    for i in range(out_ref.shape[0]):
-        out_ref[i] = padded
+    last = pad_ref[7:, :]
+    for c in range(4):
+        row = pad_ref[c : c + 1, :]
+        pad_ref[c : c + 1, :] = jnp.where(one < SLAB, row, roll(last, SLAB - 25 * c))
+    rows = pad_ref[:7, :]
+    for i in range(8):
+        many_ref[7 * i : 7 * (i + 1), :] = rows
+    many = many_ref[...]
+    for i in range(GROUP // 8):
+        out_ref[56 * i : 56 * (i + 1), :] = many
 
 
 def filter_kernel(
@@ -292,16 +360,16 @@
     field_ref,
     kinetic_ref,
     smooth_ref,
+    weight_ref,
     slabs_ref,
-    second_ref,
-    first_ref,
-    x_magic_ref,
-    x_back_ref,
+    x_half_ref,
+    x_half_back_ref,
     y_all_ref,
     y_back_ref,
     out_ref,
     potential_ref,
-    weight_ref,
+    x_magic_ref,
+    x_back_ref,
     term_ref,
     wave_ref,
     kin_ref,
@@ -309,10 +377,15 @@
     parts_ref,
     owned_ref,
 ):
-    x_weights(vector_ref, second_ref, first_ref, weight_ref)
+    for i in range(2):
+        x_magic_ref[i] = both_halves(x_half_ref[i])
+        x_back_ref[i] = both_halves(x_half_back_ref[i])
     lane = lanes_of(16)
-    for z in range(NZ):
-        slabs = [slabs_ref[pl.ds(8 * s + z, 16, stride=32), :] for s in range(4)]
+    planes = [
+        [slabs_ref[pl.ds(7 * s + z, 16, stride=28), :] for s in range(4)] for z in range(NZ - 1)
+    ]
+    planes.append([last_plane(lane, [planes[c][s] for c in range(4)]) for s in range(4)])
+    for z, slabs in enumerate(planes):
         for t in range(5):
             if t == 0:
                 row = slabs[0]
@@ -383,11 +456,11 @@
             out_ref[pl.ds(5 * q + t, GROUP, stride=25), :] = compose(lane, parts)
 
 
-def gram_kernel(rank_ref, count_ref, slot_ref, in_ref, stack_ref, out_ref, chosen_ref):
+def gram_kernel(axes, count_ref, slot_ref, in_ref, stack_ref, out_ref, chosen_ref):
     orbitals = slot_ref.shape[0]
     for i in range(orbitals):
         chosen_ref[pl.ds(i, 25, stride=orbitals), :] = in_ref[pl.ds(25 * slot_ref[i], 25), :]
-    limit = 2 * NX * count_ref[rank_ref[0]]
+    limit = 2 * NX * count_ref[lax.axis_index(axes) if axes else 0]
     lane = lanes_of(orbitals)
     total = jnp.zeros((2 * orbitals, WIDE), jnp.float32)
     empty = jnp.zeros((64 - orbitals, LANES), jnp.bfloat16)
@@ -483,7 +556,7 @@
 
 
 def call(body, kinds, outs, scratch=(), limit=48):
-    spaces = {"s": pltpu.SMEM, "v": pltpu.VMEM}
+    spaces = {"s": pltpu.SMEM, "v": pltpu.VMEM, "h": pltpu.HBM}
     many = isinstance(outs, (list, tuple))
     one = pl.BlockSpec(memory_space=pltpu.VMEM)
     return pl.pallas_call(
@@ -496,25 +569,34 @@
     )
 
 
-def field_scratch():
-    return pltpu.VMEM((ROWS, WIDE), jnp.float32)
-
-
-def run_density(rank, weight, occupation, slots, vector, linear, table):
+def vmem(*shape, dtype=jnp.float32):
+    return pltpu.VMEM(shape, dtype)
+
+
+def run_density(axes, weight, occupation, slots, vector, linear, table):
     field = shaped((ROWS, WIDE))
+    tables = [table[name] for name in ("x_kinetic", "x_magic", "y_all")]
     return call(
-        density_kernel,
-        "sssssvvvvv",
-        (field, field, field, shaped((GROUP * NZ, LANES))),
+        functools.partial(density_kernel, axes),
+        "hhhhhhhh",
+        (field, field, field, shaped((2, WIDE, WIDE), jnp.bfloat16), shaped((GROUP * 7, LANES))),
         (
-            pltpu.VMEM((2, ROWS, LANES), jnp.float32),
-            pltpu.VMEM((2, WIDE, WIDE), jnp.bfloat16),
-            pltpu.VMEM((ROWS, LANES), jnp.float32),
+            pltpu.SMEM(weight.shape, weight.dtype),
+            pltpu.SMEM(occupation.shape, occupation.dtype),
+            pltpu.SMEM(slots.shape, slots.dtype),
+            pltpu.SMEM(vector.shape, vector.dtype),
+            vmem(*linear.shape),
+            *(vmem(*t.shape, dtype=t.dtype) for t in tables),
+            vmem(2, ROWS, LANES),
+            vmem(2, WIDE, WIDE, dtype=jnp.bfloat16),
+            vmem(ROWS, LANES),
+            pltpu.SemaphoreType.DMA((8,)),
         ),
-    )(
-        rank, weight, occupation, slots, vector, linear,
-        table["x_second"], table["x_first"], table["x_magic"], table["y_all"],
-    )
+    )(weight, occupation, slots, vector, linear, *tables)
+
+
+def run_first_total(values, count):
+    return call(first_total_kernel, "v", shaped((count, NZ, LANES)))(values)
 
 
 def run_total(values, count):
@@ -525,41 +607,36 @@
     return call(
         potential_kernel,
         "vvv",
-        (shaped(external.shape), shaped((GROUP, NZ, LANES))),
-        (pltpu.VMEM((NZ, LANES), jnp.float32),),
+        (shaped(external.shape), shaped((GROUP * 7, LANES))),
+        (vmem(NZ, LANES), vmem(56, LANES)),
     )(values, external, core)
 
 
-def run_filter(counts, vector, field, kinetic, smooth, slabs, table):
+def run_filter(counts, vector, field, kinetic, smooth, weights, slabs, table):
+    tables = [table[name] for name in ("x_magic", "x_back", "y_all", "y_back")]
     return call(
         filter_kernel,
-        "ssvvvvvvvvvv",
+        "ssvvvvvvvvv",
         shaped((GROUP * 25, LANES)),
         (
-            pltpu.VMEM((ROWS, LANES), jnp.float32),
-            pltpu.VMEM((2, WIDE, WIDE), jnp.bfloat16),
-            field_scratch(),
-            field_scratch(),
-            field_scratch(),
-            field_scratch(),
-            pltpu.VMEM((2, ROWS + 24, LANES), jnp.float32),
-            pltpu.VMEM((2, GROUP * 24, LANES), jnp.float32),
+            vmem(ROWS, LANES),
+            vmem(2, WIDE, WIDE, dtype=jnp.bfloat16),
+            vmem(2, WIDE, WIDE, dtype=jnp.bfloat16),
+            *(vmem(ROWS, WIDE) for _ in range(4)),
+            vmem(2, ROWS + 24, LANES),
+            vmem(2, GROUP * 24, LANES),
         ),
-    )(
-        counts, vector, field, kinetic, smooth, slabs,
-        table["x_second"], table["x_first"], table["x_magic"], table["x_magic_back"],
-        table["y_all"], table["y_back"],
-    )
-
-
-def run_gram(rank, counts, slots, received):
+    )(counts, vector, field, kinetic, smooth, weights, slabs, *tables)
+
+
+def run_gram(axes, counts, slots, received):
     orbitals = slots.shape[0]
     return call(
-        gram_kernel,
-        "sssv",
+        functools.partial(gram_kernel, axes),
+        "ssv",
         (shaped((25, WIDE, LANES), jnp.bfloat16), shaped((8, orbitals // 2, LANES))),
-        (pltpu.VMEM((25 * orbitals, LANES), jnp.float32),),
-    )(rank, counts, slots, received)
+        (vmem(25 * orbitals, LANES),),
+    )(counts, slots, received)
 
 
 def run_rotate(values, stack, orbitals):
@@ -581,19 +658,20 @@
     core_density,
 ):
     kpt, orb = ("kpt",), ("orb_y", "orb_z")
-    rank = lax.axis_index(orb).astype(jnp.int32).reshape(1)
     table = {name: jnp.asarray(value) for name, value in tables().items()}
-    field, kinetic, smooth, partial_density = run_density(
-        rank, kpoint_weight, occupation, orbital_slot, kpoint_vector,
+    field, kinetic, smooth, weights, partial_density = run_density(
+        orb, kpoint_weight, occupation, orbital_slot, kpoint_vector,
         wavefunctions.reshape(-1, LANES), table,
     )
-    terms = exchange(partial_density.reshape(GROUP, NZ, LANES), orb)
-    terms = exchange(run_total(terms, 8), kpt)
+    terms = exchange(partial_density.reshape(GROUP, 7 * LANES), orb)
+    terms = exchange(run_first_total(terms.reshape(GROUP * 7, LANES), 8), kpt)
     density, slabs = run_potential(terms, external_potential, core_density)
-    slabs = exchange(slabs, orb).reshape(GROUP * NZ, LANES)
-    outgoing = run_filter(piece_rows, kpoint_vector, field, kinetic, smooth, slabs, table)
+    slabs = exchange(slabs.reshape(GROUP, 7 * LANES), orb).reshape(GROUP * 7, LANES)
+    outgoing = run_filter(
+        piece_rows, kpoint_vector, field, kinetic, smooth, weights, slabs, table
+    )
     received = exchange(outgoing.reshape(GROUP, 25 * LANES), orb).reshape(GROUP * 25, LANES)
-    stack, packed = run_gram(rank, piece_rows, orbital_slot, received)
+    stack, packed = run_gram(orb, piece_rows, orbital_slot, received)
     packed = exchange(packed, ("orb_z",))
     packed = exchange(run_total(packed, 8), ("orb_y",))
     return (density, run_rotate(packed, stack, orbital_slot.shape[0])[None])

time: 132 us -> 132 us (level)
  blocking collectives: 112 us -> 110 us
    all_to_all x6, blocking collectives: 112 us -> 110 us  [exchange(): return lax.all_to_all(values, axes, split_axis=0, concat_axis=0, tiled=True)]
    pallas_call x4 -> x5, Pallas kernels: 10.4 us -> 11.2 us  [the longest x1 4.91 us: run_filter(): call(filter_kernel, 'ssvvvvvvvvv', shaped((GROUP * 25, LANES)), (vmem(ROW...]
    unnamed x34 -> x28, local copies, waits for them, and re-layouts: 6.75 us -> 7 us
where the time goes in v3:
time: 132 us; the launch traced here: 131 us
  blocking collectives  110 us (83%)
  Pallas kernels  12.8 us (10%)
  local copies, waits for them, and re-layouts  7 us (5%)
  between operations  1.38 us (1%)
    all_to_all x6, blocking collectives, exchange(): return lax.all_to_all(values, axes, split_axis=0, concat_axis=0, tiled=True)  110 us
    unnamed x28, local copies, waits for them, and re-layouts  7 us
    pallas_call x1, Pallas kernels, run_filter(): call(filter_kernel, 'ssvvvvvvvvv', shaped((GROUP * 25, LANES)), (vmem(ROW...  4.91 us
    pallas_call x1, Pallas kernels, run_density(): call(functools.partial(density_kernel, axes), 'hhhhhhhh', (field, field,...  3.85 us

profile of v3, /device:TPU:2, one launch (start us, length us, event | category | flops | bytes accessed | tf_op | source)
XLA Modules:
  0.0 131.4 jit_solution(4914922355373444067)
XLA Ops:
  0.6 0.0 copy-start.10
  0.6 0.0 copy-start.8
  1.3 0.0 copy-start
  1.3 0.9 copy-done
  2.2 0.0 copy-start.1
  2.2 1.0 copy-done.1
  3.2 0.0 copy-start.2
  3.2 0.8 copy-done.2
  4.1 0.0 copy-start.3
  4.1 0.9 copy-done.3
  5.0 0.0 copy-start.9
  5.0 0.7 copy-done.9
  5.6 0.0 copy-start.11
  5.6 0.7 copy-done.11
  6.3 0.0 copy-start.13
  6.3 0.7 copy-done.13
  6.9 0.0 copy-start.4
  6.9 0.0 copy-start.5
  6.9 3.8 %shard_map.140 = (f32[640,256]{1,0:T(8,128)S(1)}, f32[640,256]{1,0:T(8,128)S(1)}, f32[640,256]{1,0:T(8,128)S(1)}, bf16[2,256,256]{2,1,0:T(8,128)(2,1)S(1)}, f32[448,128]{1,0:T(8,128)S(1)}) custom-call(f32[1]{0:T(128)S(6)} %copy.18.weight_k_hbm, f32[48]{0:T(128)S(1)} %copy-done.13, s32[48]{0:T(128)S(1)} %copy-done.11, f32[1,3]{1,0:T(1,128)S(1)} %copy-done.9, ...), custom_call_target="tpu_custom_call" | custom-call | tf_op jit(solution)/shard_map/pallas_call | solution.py:579
  10.8 30.7 %all_to_all.42 = f32[64,1,896]{2,1,0:T(1,128)S(1)} all-to-all(f32[64,1,896]{2,1,0:T(1,128)S(1)} %bitcast.13), channel_id=1, replica_groups=mesh['kpt'=8,'orb_y'=8,'orb_z'=8] {'orb_y','orb_z'}, dimensions={0} | all-to-all | bytes 458752 | tf_op jit(solution)/shard_map/all_to_all | solution.py:647
  41.5 8.6 %all_to_all.43.in_ref = f32[8,8,128]{2,1,0:T(8,128)S(1)} all-to-all(f32[8,8,128]{2,1,0:T(8,128)S(1)} %shard_map.141), channel_id=1, replica_groups=mesh['kpt'=8,'orb_y'=8,'orb_z'=8] {'kpt'}, dimensions={0} | all-to-all | bytes 65536 | tf_op jit(solution)/shard_map/all_to_all | solution.py:647
  50.1 0.0 copy-start.6
  50.1 0.7 copy-done.6
  50.8 0.0 copy-start.7
  50.8 0.7 copy-done.7
  51.5 0.7 shard_map.142
  52.2 18.5 %all_to_all.44 = f32[64,1,896]{2,1,0:T(1,128)S(1)} all-to-all(f32[64,1,896]{2,1,0:T(1,128)S(1)} %bitcast.14), channel_id=1, replica_groups=mesh['kpt'=8,'orb_y'=8,'orb_z'=8] {'orb_y','orb_z'}, dimensions={0} | all-to-all | bytes 458752 | tf_op jit(solution)/shard_map/all_to_all | solution.py:647
  70.6 0.0 copy-done.10
  70.6 0.0 copy-done.8
  70.6 0.0 copy-done.4
  70.6 0.0 copy-done.5
  70.7 4.9 %shard_map.143 = f32[1600,128]{1,0:T(8,128)S(1)} custom-call(s32[64]{0:T(128)S(1)} %copy-done.8, f32[1,3]{1,0:T(1,128)S(1)} %copy-done.10, f32[640,256]{1,0:T(8,128)S(1)} %get-tuple-element.13.field_ref, f32[640,256]{1,0:T(8,128)S(1)} %get-tuple-element.14.kinetic_ref, f32[640,256]{1,0:T(8,128)S(1)} %get-tuple-element.15.smooth_ref, ...), custom_call_target="tpu_custom_call" | custom-call | tf_op jit(solution)/shard_map/pallas_call | solution.py:617
  75.6 0.0 copy-start.12
  75.6 27.8 %all_to_all.45 = f32[64,1,3200]{2,1,0:T(1,128)S(1)} all-to-all(f32[64,1,3200]{2,1,0:T(1,128)S(1)} %bitcast.9), channel_id=1, replica_groups=mesh['kpt'=8,'orb_y'=8,'orb_z'=8] {'orb_y','orb_z'}, dimensions={0} | all-to-all | bytes 1638400 | tf_op jit(solution)/shard_map/all_to_all | solution.py:647
  103.4 0.0 copy-done.12
  103.4 1.8 %shard_map.144 = (bf16[25,256,128]{2,1,0:T(8,128)(2,1)S(1)}, f32[8,24,128]{2,1,0:T(8,128)S(1)}) custom-call(s32[64]{0:T(128)S(1)} %copy-done.8, s32[48]{0:T(128)S(1)} %copy-done.12, f32[1600,128]{1,0:T(8,128)S(1)} %bitcast.8), custom_call_target="tpu_custom_call" | custom-call | tf_op jit(solution)/shard_map/pallas_call | solution.py:634
  105.2 13.6 %all_to_all.46.in_ref = f32[8,24,128]{2,1,0:T(8,128)S(1)} all-to-all(f32[8,24,128]{2,1,0:T(8,128)S(1)} %get-tuple-element.18), channel_id=1, replica_groups=mesh['kpt'=8,'orb_y'=8,'orb_z'=8] {'orb_z'}, dimensions={0} | all-to-all | bytes 196608 | tf_op jit(solution)/shard_map/all_to_all | solution.py:647
  118.8 11.1 %all_to_all.47.in_ref = f32[8,24,128]{2,1,0:T(8,128)S(1)} all-to-all(f32[8,24,128]{2,1,0:T(8,128)S(1)} %shard_map.145), channel_id=1, replica_groups=mesh['kpt'=8,'orb_y'=8,'orb_z'=8] {'orb_y'}, dimensions={0} | all-to-all | bytes 196608 | tf_op jit(solution)/shard_map/all_to_all | solution.py:647
  129.9 1.6 %shard_map.146 = f32[48,3200]{1,0:T(8,128)} custom-call(f32[8,24,128]{2,1,0:T(8,128)S(1)} %all_to_all.47.in_ref, bf16[25,256,128]{2,1,0:T(8,128)(2,1)S(1)} %get-tuple-element.19.stack_ref), custom_call_target="tpu_custom_call" | custom-call | tf_op jit(solution)/shard_map/pallas_call | solution.py:643
  (2 shorter events, 0.0 us)
Async XLA Ops:
  0.6 70.0 %copy-start.10 = (f32[1,3]{1,0:T(1,128)S(1)}, f32[1,3]{1,0:T(1,128)}, u32[]{:S(2)}) copy-start(f32[1,3]{1,0:T(1,128)} %vector_ref.1) | copy-start | bytes 40
  0.6 70.0 %copy-start.8 = (s32[64]{0:T(128)S(1)}, s32[64]{0:T(128)}, u32[]{:S(2)}) copy-start(s32[64]{0:T(128)} %count_ref.3) | copy-start | bytes 772
  1.3 0.9 copy-start
  2.2 1.0 copy-start.1
  3.2 0.8 copy-start.2
  4.1 0.9 copy-start.3
  5.0 0.7 copy-start.9
  5.6 0.7 copy-start.11
  6.3 0.7 copy-start.13
  6.9 63.7 %copy-start.4 = (bf16[2,128,128]{2,1,0:T(8,128)(2,1)S(1)}, bf16[2,128,128]{2,1,0:T(8,128)(2,1)}, u32[]{:S(2)}) copy-start(bf16[2,128,128]{2,1,0:T(8,128)(2,1)} %constant.12.clone.x_half_back_ref) | copy-start | bytes 196612
  6.9 63.7 %copy-start.5 = (bf16[80,240]{1,0:T(8,128)(2,1)S(1)}, bf16[80,240]{1,0:T(8,128)(2,1)}, u32[]{:S(2)}) copy-start(bf16[80,240]{1,0:T(8,128)(2,1)} %constant.14.clone.y_back_ref) | copy-start | bytes 115204
  50.1 0.7 copy-start.6
  50.8 0.7 copy-start.7
  75.6 27.8 %copy-start.12 = (s32[48]{0:T(128)S(1)}, s32[48]{0:T(128)}, u32[]{:S(2)}) copy-start(s32[48]{0:T(128)} %slot_ref.1) | copy-start | bytes 580
